TPU v7x, 512 devices: a whole 4x4x16 slice. The times are simulated.
512 devices in a mesh: blk: 32 (over x, z_lo, core), grp: 16 (over y, z_hi).
Axes of the slice: x: 4, y: 4, z: 16 (z_hi: 4, z_lo: 4; z = z_hi * 4 + z_lo), core: 2. Of those that a mesh axis runs over, the one named last changes fastest.
Arguments:
- points: float32 [9, 65536], P(None, ('blk', 'grp')), may hold values from -6 to 6
- inv_length: float32 [9], replicated, may hold values from 0.6 to 1.2
- probes: float32 [32, 65536], P(None, ('blk', 'grp')), may hold values from -6 to 6
- noise: float32 [1], replicated, may hold values from 0.2 to 1
Outputs:
- product: float32 [32, 65536], P(None, ('blk', 'grp'))
All inputs are finite; a program needn't handle non-finite values.
Results may differ from a plain program's by a relative error of at most 0.0003.
Values sent between devices are 32-bit elements; how exact they have to be, the bound alone decides.
No kernel may reach another device: no remote copies, remote signals or barrier semaphores. Data moves between devices by JAX's collectives and lax.ppermute only.
A program may use at most 64 MiB of HBM per device.

v0:
```python
import math

import jax
import jax.numpy as jnp
from jax import lax
from jax.sharding import PartitionSpec as P

ROOT_FIVE = math.sqrt(5.0)


def from_behind(shard, axis, by):
    size = lax.axis_size(axis)
    return lax.ppermute(shard, axis, [(i, (i + by) % size) for i in range(size)])


def matern_tile(rows, cols):
    squared = jnp.zeros((rows.shape[1], cols.shape[1]), jnp.float32)
    for coord in range(rows.shape[0]):
        spread = rows[coord][:, None] - cols[coord][None, :]
        squared = squared + spread * spread
    scaled_r = ROOT_FIVE * jnp.sqrt(squared)
    return (1.0 + scaled_r + scaled_r * scaled_r / 3.0) * jnp.exp(-scaled_r)


def advance(far_points, far_probes):
    return from_behind((far_points, far_probes), "blk", 1)


def apply_tile(tile, far_probes):
    return jnp.einsum(
        "cg,pg->cp",
        far_probes,
        tile,
        preferred_element_type=jnp.float32,
        precision=lax.Precision.HIGHEST,
    )


def body(points, inv_length, probes, noise):
    scaled = points * inv_length[:, None]
    far_points, far_probes = (
        lax.all_gather(scaled, "grp", axis=1, tiled=True),
        lax.all_gather(probes, "grp", axis=1, tiled=True),
    )
    cycle_size = lax.axis_size("blk")
    result = apply_tile(matern_tile(scaled, far_points), far_probes)

    def full_step(index, carry):
        moved_points, moved_probes, total = carry
        moved_points, moved_probes = advance(moved_points, moved_probes)
        tile = matern_tile(scaled, moved_points)
        return (moved_points, moved_probes, total + apply_tile(tile, moved_probes))

    far_points, far_probes, result = lax.fori_loop(
        1, cycle_size, full_step, (far_points, far_probes, result)
    )
    return result + noise[0] * probes


def solution(mesh):
    in_specs = (P(None, ("blk", "grp")), P(), P(None, ("blk", "grp")), P())
    out_specs = P(None, ("blk", "grp"))
    return jax.shard_map(body, mesh=mesh, in_specs=in_specs, out_specs=out_specs, check_vma=False)
```

profile of v0, /device:TPU:128, one launch (start us, length us, event | category | flops | bytes accessed | tf_op | source)
XLA Modules:
  0.0 609.9 jit_solution(10359141094168705360)
XLA Ops:
  0.8 53.4 %all_gather.6 = f32[9,2048]{1,0:T(8,128)S(1)} all-gather(f32[9,128]{1,0:T(8,128)S(1)} %broadcast_multiply_fusion), channel_id=1, replica_groups=mesh['blk'=32,'grp'=16] {'grp'}, dimensions={1}, use_global_device_ids=true | all-gather | bytes 78336 | tf_op jit(solution)/shard_map/all_gather | solution.py:42
  55.0 51.8 %all_gather.7 = f32[32,2048]{1,0:T(8,128)S(1)} all-gather(f32[32,128]{1,0:T(8,128)S(1)} %copy-done), channel_id=1, replica_groups=mesh['blk'=32,'grp'=16] {'grp'}, dimensions={1}, use_global_device_ids=true | all-gather | bytes 278528 | tf_op jit(solution)/shard_map/all_gather | solution.py:43
  109.4 499.3 %while.14 = (s32[]{:T(128)}, f32[9,2048]{1,0:T(8,128)S(1)}, f32[32,2048]{1,0:T(8,128)S(1)}, f32[32,128]{1,0:T(8,128)S(1)}, f32[9,128]{1,0:T(8,128)S(1)}, /*index=5*/s32[]{:T(128)}) while((s32[]{:T(128)}, f32[9,2048]{1,0:T(8,128)S(1)}, f32[32,2048]{1,0:T(8,128)S(1)}, f32[32,128]{1,0:T(8,128)S(1)}, f32[9,128]{1,0:T(8,128)S(1)}, ...), condition=%wide.region_1.0_spmd, body=%wide.region_0.0_spmd.sunk | while | flops 109318144 | bytes 2545301 | solution.py:54
  113.7 5.8 collective-permute-done
  119.6 3.3 collective-permute-done.1
  129.4 6.3 %collective-permute-done = f32[9,2048]{1,0:T(8,128)S(1)} collective-permute-done((f32[9,2048]{1,0:T(8,128)S(1)}, f32[9,2048]{1,0:T(8,128)S(1)}, u32[]{:S(2)}, u32[]{:S(2)}) %collective-permute-start) | collective-permute-done | bytes 73760 | tf_op jit(solution)/shard_map/while/body/eval_jaxpr/ppermute | solution.py:13
  135.7 3.3 collective-permute-done.1
  145.5 6.3 %collective-permute-done = f32[9,2048]{1,0:T(8,128)S(1)} collective-permute-done((f32[9,2048]{1,0:T(8,128)S(1)}, f32[9,2048]{1,0:T(8,128)S(1)}, u32[]{:S(2)}, u32[]{:S(2)}) %collective-permute-start) | collective-permute-done | bytes 73760 | tf_op jit(solution)/shard_map/while/body/eval_jaxpr/ppermute | solution.py:13
  151.9 3.3 collective-permute-done.1
  161.6 6.3 %collective-permute-done = f32[9,2048]{1,0:T(8,128)S(1)} collective-permute-done((f32[9,2048]{1,0:T(8,128)S(1)}, f32[9,2048]{1,0:T(8,128)S(1)}, u32[]{:S(2)}, u32[]{:S(2)}) %collective-permute-start) | collective-permute-done | bytes 73760 | tf_op jit(solution)/shard_map/while/body/eval_jaxpr/ppermute | solution.py:13
  168.0 3.3 collective-permute-done.1
  177.7 6.3 %collective-permute-done = f32[9,2048]{1,0:T(8,128)S(1)} collective-permute-done((f32[9,2048]{1,0:T(8,128)S(1)}, f32[9,2048]{1,0:T(8,128)S(1)}, u32[]{:S(2)}, u32[]{:S(2)}) %collective-permute-start) | collective-permute-done | bytes 73760 | tf_op jit(solution)/shard_map/while/body/eval_jaxpr/ppermute | solution.py:13
  184.1 3.3 collective-permute-done.1
  193.8 6.3 %collective-permute-done = f32[9,2048]{1,0:T(8,128)S(1)} collective-permute-done((f32[9,2048]{1,0:T(8,128)S(1)}, f32[9,2048]{1,0:T(8,128)S(1)}, u32[]{:S(2)}, u32[]{:S(2)}) %collective-permute-start) | collective-permute-done | bytes 73760 | tf_op jit(solution)/shard_map/while/body/eval_jaxpr/ppermute | solution.py:13
  200.2 3.3 collective-permute-done.1
  209.9 6.3 %collective-permute-done = f32[9,2048]{1,0:T(8,128)S(1)} collective-permute-done((f32[9,2048]{1,0:T(8,128)S(1)}, f32[9,2048]{1,0:T(8,128)S(1)}, u32[]{:S(2)}, u32[]{:S(2)}) %collective-permute-start) | collective-permute-done | bytes 73760 | tf_op jit(solution)/shard_map/while/body/eval_jaxpr/ppermute | solution.py:13
  216.3 3.3 collective-permute-done.1
  226.0 6.3 %collective-permute-done = f32[9,2048]{1,0:T(8,128)S(1)} collective-permute-done((f32[9,2048]{1,0:T(8,128)S(1)}, f32[9,2048]{1,0:T(8,128)S(1)}, u32[]{:S(2)}, u32[]{:S(2)}) %collective-permute-start) | collective-permute-done | bytes 73760 | tf_op jit(solution)/shard_map/while/body/eval_jaxpr/ppermute | solution.py:13
  232.4 3.3 collective-permute-done.1
  242.1 6.3 %collective-permute-done = f32[9,2048]{1,0:T(8,128)S(1)} collective-permute-done((f32[9,2048]{1,0:T(8,128)S(1)}, f32[9,2048]{1,0:T(8,128)S(1)}, u32[]{:S(2)}, u32[]{:S(2)}) %collective-permute-start) | collective-permute-done | bytes 73760 | tf_op jit(solution)/shard_map/while/body/eval_jaxpr/ppermute | solution.py:13
  248.5 3.3 collective-permute-done.1
  258.2 6.3 %collective-permute-done = f32[9,2048]{1,0:T(8,128)S(1)} collective-permute-done((f32[9,2048]{1,0:T(8,128)S(1)}, f32[9,2048]{1,0:T(8,128)S(1)}, u32[]{:S(2)}, u32[]{:S(2)}) %collective-permute-start) | collective-permute-done | bytes 73760 | tf_op jit(solution)/shard_map/while/body/eval_jaxpr/ppermute | solution.py:13
  264.6 3.3 collective-permute-done.1
  274.3 6.3 %collective-permute-done = f32[9,2048]{1,0:T(8,128)S(1)} collective-permute-done((f32[9,2048]{1,0:T(8,128)S(1)}, f32[9,2048]{1,0:T(8,128)S(1)}, u32[]{:S(2)}, u32[]{:S(2)}) %collective-permute-start) | collective-permute-done | bytes 73760 | tf_op jit(solution)/shard_map/while/body/eval_jaxpr/ppermute | solution.py:13
  280.7 3.3 collective-permute-done.1
  290.4 6.3 %collective-permute-done = f32[9,2048]{1,0:T(8,128)S(1)} collective-permute-done((f32[9,2048]{1,0:T(8,128)S(1)}, f32[9,2048]{1,0:T(8,128)S(1)}, u32[]{:S(2)}, u32[]{:S(2)}) %collective-permute-start) | collective-permute-done | bytes 73760 | tf_op jit(solution)/shard_map/while/body/eval_jaxpr/ppermute | solution.py:13
  296.8 3.3 collective-permute-done.1
  306.5 6.3 %collective-permute-done = f32[9,2048]{1,0:T(8,128)S(1)} collective-permute-done((f32[9,2048]{1,0:T(8,128)S(1)}, f32[9,2048]{1,0:T(8,128)S(1)}, u32[]{:S(2)}, u32[]{:S(2)}) %collective-permute-start) | collective-permute-done | bytes 73760 | tf_op jit(solution)/shard_map/while/body/eval_jaxpr/ppermute | solution.py:13
  312.9 3.3 collective-permute-done.1
  322.6 6.3 %collective-permute-done = f32[9,2048]{1,0:T(8,128)S(1)} collective-permute-done((f32[9,2048]{1,0:T(8,128)S(1)}, f32[9,2048]{1,0:T(8,128)S(1)}, u32[]{:S(2)}, u32[]{:S(2)}) %collective-permute-start) | collective-permute-done | bytes 73760 | tf_op jit(solution)/shard_map/while/body/eval_jaxpr/ppermute | solution.py:13
  329.0 3.3 collective-permute-done.1
  338.7 6.3 %collective-permute-done = f32[9,2048]{1,0:T(8,128)S(1)} collective-permute-done((f32[9,2048]{1,0:T(8,128)S(1)}, f32[9,2048]{1,0:T(8,128)S(1)}, u32[]{:S(2)}, u32[]{:S(2)}) %collective-permute-start) | collective-permute-done | bytes 73760 | tf_op jit(solution)/shard_map/while/body/eval_jaxpr/ppermute | solution.py:13
  345.1 3.3 collective-permute-done.1
  354.8 6.3 %collective-permute-done = f32[9,2048]{1,0:T(8,128)S(1)} collective-permute-done((f32[9,2048]{1,0:T(8,128)S(1)}, f32[9,2048]{1,0:T(8,128)S(1)}, u32[]{:S(2)}, u32[]{:S(2)}) %collective-permute-start) | collective-permute-done | bytes 73760 | tf_op jit(solution)/shard_map/while/body/eval_jaxpr/ppermute | solution.py:13
  361.2 3.3 collective-permute-done.1
  370.9 6.3 %collective-permute-done = f32[9,2048]{1,0:T(8,128)S(1)} collective-permute-done((f32[9,2048]{1,0:T(8,128)S(1)}, f32[9,2048]{1,0:T(8,128)S(1)}, u32[]{:S(2)}, u32[]{:S(2)}) %collective-permute-start) | collective-permute-done | bytes 73760 | tf_op jit(solution)/shard_map/while/body/eval_jaxpr/ppermute | solution.py:13
  377.3 3.3 collective-permute-done.1
  387.0 6.3 %collective-permute-done = f32[9,2048]{1,0:T(8,128)S(1)} collective-permute-done((f32[9,2048]{1,0:T(8,128)S(1)}, f32[9,2048]{1,0:T(8,128)S(1)}, u32[]{:S(2)}, u32[]{:S(2)}) %collective-permute-start) | collective-permute-done | bytes 73760 | tf_op jit(solution)/shard_map/while/body/eval_jaxpr/ppermute | solution.py:13
  393.4 3.3 collective-permute-done.1
  403.2 6.3 %collective-permute-done = f32[9,2048]{1,0:T(8,128)S(1)} collective-permute-done((f32[9,2048]{1,0:T(8,128)S(1)}, f32[9,2048]{1,0:T(8,128)S(1)}, u32[]{:S(2)}, u32[]{:S(2)}) %collective-permute-start) | collective-permute-done | bytes 73760 | tf_op jit(solution)/shard_map/while/body/eval_jaxpr/ppermute | solution.py:13
  409.5 3.3 collective-permute-done.1
  419.3 6.3 %collective-permute-done = f32[9,2048]{1,0:T(8,128)S(1)} collective-permute-done((f32[9,2048]{1,0:T(8,128)S(1)}, f32[9,2048]{1,0:T(8,128)S(1)}, u32[]{:S(2)}, u32[]{:S(2)}) %collective-permute-start) | collective-permute-done | bytes 73760 | tf_op jit(solution)/shard_map/while/body/eval_jaxpr/ppermute | solution.py:13
  425.7 3.3 collective-permute-done.1
  435.4 6.3 %collective-permute-done = f32[9,2048]{1,0:T(8,128)S(1)} collective-permute-done((f32[9,2048]{1,0:T(8,128)S(1)}, f32[9,2048]{1,0:T(8,128)S(1)}, u32[]{:S(2)}, u32[]{:S(2)}) %collective-permute-start) | collective-permute-done | bytes 73760 | tf_op jit(solution)/shard_map/while/body/eval_jaxpr/ppermute | solution.py:13
  441.8 3.3 collective-permute-done.1
  451.5 6.3 %collective-permute-done = f32[9,2048]{1,0:T(8,128)S(1)} collective-permute-done((f32[9,2048]{1,0:T(8,128)S(1)}, f32[9,2048]{1,0:T(8,128)S(1)}, u32[]{:S(2)}, u32[]{:S(2)}) %collective-permute-start) | collective-permute-done | bytes 73760 | tf_op jit(solution)/shard_map/while/body/eval_jaxpr/ppermute | solution.py:13
  457.9 3.3 collective-permute-done.1
  467.6 6.3 %collective-permute-done = f32[9,2048]{1,0:T(8,128)S(1)} collective-permute-done((f32[9,2048]{1,0:T(8,128)S(1)}, f32[9,2048]{1,0:T(8,128)S(1)}, u32[]{:S(2)}, u32[]{:S(2)}) %collective-permute-start) | collective-permute-done | bytes 73760 | tf_op jit(solution)/shard_map/while/body/eval_jaxpr/ppermute | solution.py:13
  474.0 3.3 collective-permute-done.1
  483.7 6.3 %collective-permute-done = f32[9,2048]{1,0:T(8,128)S(1)} collective-permute-done((f32[9,2048]{1,0:T(8,128)S(1)}, f32[9,2048]{1,0:T(8,128)S(1)}, u32[]{:S(2)}, u32[]{:S(2)}) %collective-permute-start) | collective-permute-done | bytes 73760 | tf_op jit(solution)/shard_map/while/body/eval_jaxpr/ppermute | solution.py:13
  490.1 3.3 collective-permute-done.1
  499.8 6.3 %collective-permute-done = f32[9,2048]{1,0:T(8,128)S(1)} collective-permute-done((f32[9,2048]{1,0:T(8,128)S(1)}, f32[9,2048]{1,0:T(8,128)S(1)}, u32[]{:S(2)}, u32[]{:S(2)}) %collective-permute-start) | collective-permute-done | bytes 73760 | tf_op jit(solution)/shard_map/while/body/eval_jaxpr/ppermute | solution.py:13
  506.2 3.3 collective-permute-done.1
  515.9 6.3 %collective-permute-done = f32[9,2048]{1,0:T(8,128)S(1)} collective-permute-done((f32[9,2048]{1,0:T(8,128)S(1)}, f32[9,2048]{1,0:T(8,128)S(1)}, u32[]{:S(2)}, u32[]{:S(2)}) %collective-permute-start) | collective-permute-done | bytes 73760 | tf_op jit(solution)/shard_map/while/body/eval_jaxpr/ppermute | solution.py:13
  522.3 3.3 collective-permute-done.1
  532.0 6.3 %collective-permute-done = f32[9,2048]{1,0:T(8,128)S(1)} collective-permute-done((f32[9,2048]{1,0:T(8,128)S(1)}, f32[9,2048]{1,0:T(8,128)S(1)}, u32[]{:S(2)}, u32[]{:S(2)}) %collective-permute-start) | collective-permute-done | bytes 73760 | tf_op jit(solution)/shard_map/while/body/eval_jaxpr/ppermute | solution.py:13
  538.4 3.3 collective-permute-done.1
  548.1 6.3 %collective-permute-done = f32[9,2048]{1,0:T(8,128)S(1)} collective-permute-done((f32[9,2048]{1,0:T(8,128)S(1)}, f32[9,2048]{1,0:T(8,128)S(1)}, u32[]{:S(2)}, u32[]{:S(2)}) %collective-permute-start) | collective-permute-done | bytes 73760 | tf_op jit(solution)/shard_map/while/body/eval_jaxpr/ppermute | solution.py:13
  554.5 3.3 collective-permute-done.1
  564.2 6.3 %collective-permute-done = f32[9,2048]{1,0:T(8,128)S(1)} collective-permute-done((f32[9,2048]{1,0:T(8,128)S(1)}, f32[9,2048]{1,0:T(8,128)S(1)}, u32[]{:S(2)}, u32[]{:S(2)}) %collective-permute-start) | collective-permute-done | bytes 73760 | tf_op jit(solution)/shard_map/while/body/eval_jaxpr/ppermute | solution.py:13
  580.3 6.3 %collective-permute-done = f32[9,2048]{1,0:T(8,128)S(1)} collective-permute-done((f32[9,2048]{1,0:T(8,128)S(1)}, f32[9,2048]{1,0:T(8,128)S(1)}, u32[]{:S(2)}, u32[]{:S(2)}) %collective-permute-start) | collective-permute-done | bytes 73760 | tf_op jit(solution)/shard_map/while/body/eval_jaxpr/ppermute | solution.py:13
  586.7 3.3 collective-permute-done.1
  596.4 6.3 %collective-permute-done = f32[9,2048]{1,0:T(8,128)S(1)} collective-permute-done((f32[9,2048]{1,0:T(8,128)S(1)}, f32[9,2048]{1,0:T(8,128)S(1)}, u32[]{:S(2)}, u32[]{:S(2)}) %collective-permute-start) | collective-permute-done | bytes 73760 | tf_op jit(solution)/shard_map/while/body/eval_jaxpr/ppermute | solution.py:13
  602.8 3.3 collective-permute-done.1
  (225 shorter events, 208.8 us)
Async XLA Ops:
  54.3 0.7 copy-start
  109.4 10.2 %collective-permute-start = (f32[9,2048]{1,0:T(8,128)S(1)}, f32[9,2048]{1,0:T(8,128)S(1)}, u32[]{:S(2)}, u32[]{:S(2)}) collective-permute-start(f32[9,2048]{1,0:T(8,128)S(1)} %get-tuple-element.153), channel_id=1, source_target_pairs={{0,16},{16,32},{32,48},{48,64},{64,80},{80,96},{96,112},{112,128},... | collective-permute-start | bytes 221192 | tf_op jit(solution)/shard_map/while/body/eval_jaxpr/ppermute | solution.py:13
  111.3 11.6 %collective-permute-start.1 = (f32[32,2048]{1,0:T(8,128)S(1)}, f32[32,2048]{1,0:T(8,128)S(1)}, u32[]{:S(2)}, u32[]{:S(2)}) collective-permute-start(f32[32,2048]{1,0:T(8,128)S(1)} %get-tuple-element.154), channel_id=1, source_target_pairs={{0,16},{16,32},{32,48},{48,64},{64,80},{80,96},{96,112},{112,128},... | collective-permute-start | bytes 786440 | tf_op jit(solution)/shard_map/while/body/eval_jaxpr/ppermute | solution.py:13
  125.5 10.2 %collective-permute-start = (f32[9,2048]{1,0:T(8,128)S(1)}, f32[9,2048]{1,0:T(8,128)S(1)}, u32[]{:S(2)}, u32[]{:S(2)}) collective-permute-start(f32[9,2048]{1,0:T(8,128)S(1)} %get-tuple-element.153), channel_id=1, source_target_pairs={{0,16},{16,32},{32,48},{48,64},{64,80},{80,96},{96,112},{112,128},... | collective-permute-start | bytes 221192 | tf_op jit(solution)/shard_map/while/body/eval_jaxpr/ppermute | solution.py:13
  127.4 11.6 %collective-permute-start.1 = (f32[32,2048]{1,0:T(8,128)S(1)}, f32[32,2048]{1,0:T(8,128)S(1)}, u32[]{:S(2)}, u32[]{:S(2)}) collective-permute-start(f32[32,2048]{1,0:T(8,128)S(1)} %get-tuple-element.154), channel_id=1, source_target_pairs={{0,16},{16,32},{32,48},{48,64},{64,80},{80,96},{96,112},{112,128},... | collective-permute-start | bytes 786440 | tf_op jit(solution)/shard_map/while/body/eval_jaxpr/ppermute | solution.py:13
  141.6 10.2 %collective-permute-start = (f32[9,2048]{1,0:T(8,128)S(1)}, f32[9,2048]{1,0:T(8,128)S(1)}, u32[]{:S(2)}, u32[]{:S(2)}) collective-permute-start(f32[9,2048]{1,0:T(8,128)S(1)} %get-tuple-element.153), channel_id=1, source_target_pairs={{0,16},{16,32},{32,48},{48,64},{64,80},{80,96},{96,112},{112,128},... | collective-permute-start | bytes 221192 | tf_op jit(solution)/shard_map/while/body/eval_jaxpr/ppermute | solution.py:13
  143.5 11.6 %collective-permute-start.1 = (f32[32,2048]{1,0:T(8,128)S(1)}, f32[32,2048]{1,0:T(8,128)S(1)}, u32[]{:S(2)}, u32[]{:S(2)}) collective-permute-start(f32[32,2048]{1,0:T(8,128)S(1)} %get-tuple-element.154), channel_id=1, source_target_pairs={{0,16},{16,32},{32,48},{48,64},{64,80},{80,96},{96,112},{112,128},... | collective-permute-start | bytes 786440 | tf_op jit(solution)/shard_map/while/body/eval_jaxpr/ppermute | solution.py:13
  157.7 10.2 %collective-permute-start = (f32[9,2048]{1,0:T(8,128)S(1)}, f32[9,2048]{1,0:T(8,128)S(1)}, u32[]{:S(2)}, u32[]{:S(2)}) collective-permute-start(f32[9,2048]{1,0:T(8,128)S(1)} %get-tuple-element.153), channel_id=1, source_target_pairs={{0,16},{16,32},{32,48},{48,64},{64,80},{80,96},{96,112},{112,128},... | collective-permute-start | bytes 221192 | tf_op jit(solution)/shard_map/while/body/eval_jaxpr/ppermute | solution.py:13
  159.6 11.6 %collective-permute-start.1 = (f32[32,2048]{1,0:T(8,128)S(1)}, f32[32,2048]{1,0:T(8,128)S(1)}, u32[]{:S(2)}, u32[]{:S(2)}) collective-permute-start(f32[32,2048]{1,0:T(8,128)S(1)} %get-tuple-element.154), channel_id=1, source_target_pairs={{0,16},{16,32},{32,48},{48,64},{64,80},{80,96},{96,112},{112,128},... | collective-permute-start | bytes 786440 | tf_op jit(solution)/shard_map/while/body/eval_jaxpr/ppermute | solution.py:13
  173.8 10.2 %collective-permute-start = (f32[9,2048]{1,0:T(8,128)S(1)}, f32[9,2048]{1,0:T(8,128)S(1)}, u32[]{:S(2)}, u32[]{:S(2)}) collective-permute-start(f32[9,2048]{1,0:T(8,128)S(1)} %get-tuple-element.153), channel_id=1, source_target_pairs={{0,16},{16,32},{32,48},{48,64},{64,80},{80,96},{96,112},{112,128},... | collective-permute-start | bytes 221192 | tf_op jit(solution)/shard_map/while/body/eval_jaxpr/ppermute | solution.py:13
  175.7 11.6 %collective-permute-start.1 = (f32[32,2048]{1,0:T(8,128)S(1)}, f32[32,2048]{1,0:T(8,128)S(1)}, u32[]{:S(2)}, u32[]{:S(2)}) collective-permute-start(f32[32,2048]{1,0:T(8,128)S(1)} %get-tuple-element.154), channel_id=1, source_target_pairs={{0,16},{16,32},{32,48},{48,64},{64,80},{80,96},{96,112},{112,128},... | collective-permute-start | bytes 786440 | tf_op jit(solution)/shard_map/while/body/eval_jaxpr/ppermute | solution.py:13
  189.9 10.2 %collective-permute-start = (f32[9,2048]{1,0:T(8,128)S(1)}, f32[9,2048]{1,0:T(8,128)S(1)}, u32[]{:S(2)}, u32[]{:S(2)}) collective-permute-start(f32[9,2048]{1,0:T(8,128)S(1)} %get-tuple-element.153), channel_id=1, source_target_pairs={{0,16},{16,32},{32,48},{48,64},{64,80},{80,96},{96,112},{112,128},... | collective-permute-start | bytes 221192 | tf_op jit(solution)/shard_map/while/body/eval_jaxpr/ppermute | solution.py:13
  191.8 11.6 %collective-permute-start.1 = (f32[32,2048]{1,0:T(8,128)S(1)}, f32[32,2048]{1,0:T(8,128)S(1)}, u32[]{:S(2)}, u32[]{:S(2)}) collective-permute-start(f32[32,2048]{1,0:T(8,128)S(1)} %get-tuple-element.154), channel_id=1, source_target_pairs={{0,16},{16,32},{32,48},{48,64},{64,80},{80,96},{96,112},{112,128},... | collective-permute-start | bytes 786440 | tf_op jit(solution)/shard_map/while/body/eval_jaxpr/ppermute | solution.py:13
  206.0 10.2 %collective-permute-start = (f32[9,2048]{1,0:T(8,128)S(1)}, f32[9,2048]{1,0:T(8,128)S(1)}, u32[]{:S(2)}, u32[]{:S(2)}) collective-permute-start(f32[9,2048]{1,0:T(8,128)S(1)} %get-tuple-element.153), channel_id=1, source_target_pairs={{0,16},{16,32},{32,48},{48,64},{64,80},{80,96},{96,112},{112,128},... | collective-permute-start | bytes 221192 | tf_op jit(solution)/shard_map/while/body/eval_jaxpr/ppermute | solution.py:13
  207.9 11.6 %collective-permute-start.1 = (f32[32,2048]{1,0:T(8,128)S(1)}, f32[32,2048]{1,0:T(8,128)S(1)}, u32[]{:S(2)}, u32[]{:S(2)}) collective-permute-start(f32[32,2048]{1,0:T(8,128)S(1)} %get-tuple-element.154), channel_id=1, source_target_pairs={{0,16},{16,32},{32,48},{48,64},{64,80},{80,96},{96,112},{112,128},... | collective-permute-start | bytes 786440 | tf_op jit(solution)/shard_map/while/body/eval_jaxpr/ppermute | solution.py:13
  222.1 10.2 %collective-permute-start = (f32[9,2048]{1,0:T(8,128)S(1)}, f32[9,2048]{1,0:T(8,128)S(1)}, u32[]{:S(2)}, u32[]{:S(2)}) collective-permute-start(f32[9,2048]{1,0:T(8,128)S(1)} %get-tuple-element.153), channel_id=1, source_target_pairs={{0,16},{16,32},{32,48},{48,64},{64,80},{80,96},{96,112},{112,128},... | collective-permute-start | bytes 221192 | tf_op jit(solution)/shard_map/while/body/eval_jaxpr/ppermute | solution.py:13
  224.0 11.6 %collective-permute-start.1 = (f32[32,2048]{1,0:T(8,128)S(1)}, f32[32,2048]{1,0:T(8,128)S(1)}, u32[]{:S(2)}, u32[]{:S(2)}) collective-permute-start(f32[32,2048]{1,0:T(8,128)S(1)} %get-tuple-element.154), channel_id=1, source_target_pairs={{0,16},{16,32},{32,48},{48,64},{64,80},{80,96},{96,112},{112,128},... | collective-permute-start | bytes 786440 | tf_op jit(solution)/shard_map/while/body/eval_jaxpr/ppermute | solution.py:13
  238.2 10.2 %collective-permute-start = (f32[9,2048]{1,0:T(8,128)S(1)}, f32[9,2048]{1,0:T(8,128)S(1)}, u32[]{:S(2)}, u32[]{:S(2)}) collective-permute-start(f32[9,2048]{1,0:T(8,128)S(1)} %get-tuple-element.153), channel_id=1, source_target_pairs={{0,16},{16,32},{32,48},{48,64},{64,80},{80,96},{96,112},{112,128},... | collective-permute-start | bytes 221192 | tf_op jit(solution)/shard_map/while/body/eval_jaxpr/ppermute | solution.py:13
  240.1 11.6 %collective-permute-start.1 = (f32[32,2048]{1,0:T(8,128)S(1)}, f32[32,2048]{1,0:T(8,128)S(1)}, u32[]{:S(2)}, u32[]{:S(2)}) collective-permute-start(f32[32,2048]{1,0:T(8,128)S(1)} %get-tuple-element.154), channel_id=1, source_target_pairs={{0,16},{16,32},{32,48},{48,64},{64,80},{80,96},{96,112},{112,128},... | collective-permute-start | bytes 786440 | tf_op jit(solution)/shard_map/while/body/eval_jaxpr/ppermute | solution.py:13
  254.3 10.2 %collective-permute-start = (f32[9,2048]{1,0:T(8,128)S(1)}, f32[9,2048]{1,0:T(8,128)S(1)}, u32[]{:S(2)}, u32[]{:S(2)}) collective-permute-start(f32[9,2048]{1,0:T(8,128)S(1)} %get-tuple-element.153), channel_id=1, source_target_pairs={{0,16},{16,32},{32,48},{48,64},{64,80},{80,96},{96,112},{112,128},... | collective-permute-start | bytes 221192 | tf_op jit(solution)/shard_map/while/body/eval_jaxpr/ppermute | solution.py:13
  256.3 11.6 %collective-permute-start.1 = (f32[32,2048]{1,0:T(8,128)S(1)}, f32[32,2048]{1,0:T(8,128)S(1)}, u32[]{:S(2)}, u32[]{:S(2)}) collective-permute-start(f32[32,2048]{1,0:T(8,128)S(1)} %get-tuple-element.154), channel_id=1, source_target_pairs={{0,16},{16,32},{32,48},{48,64},{64,80},{80,96},{96,112},{112,128},... | collective-permute-start | bytes 786440 | tf_op jit(solution)/shard_map/while/body/eval_jaxpr/ppermute | solution.py:13
  270.4 10.2 %collective-permute-start = (f32[9,2048]{1,0:T(8,128)S(1)}, f32[9,2048]{1,0:T(8,128)S(1)}, u32[]{:S(2)}, u32[]{:S(2)}) collective-permute-start(f32[9,2048]{1,0:T(8,128)S(1)} %get-tuple-element.153), channel_id=1, source_target_pairs={{0,16},{16,32},{32,48},{48,64},{64,80},{80,96},{96,112},{112,128},... | collective-permute-start | bytes 221192 | tf_op jit(solution)/shard_map/while/body/eval_jaxpr/ppermute | solution.py:13
  272.4 11.6 %collective-permute-start.1 = (f32[32,2048]{1,0:T(8,128)S(1)}, f32[32,2048]{1,0:T(8,128)S(1)}, u32[]{:S(2)}, u32[]{:S(2)}) collective-permute-start(f32[32,2048]{1,0:T(8,128)S(1)} %get-tuple-element.154), channel_id=1, source_target_pairs={{0,16},{16,32},{32,48},{48,64},{64,80},{80,96},{96,112},{112,128},... | collective-permute-start | bytes 786440 | tf_op jit(solution)/shard_map/while/body/eval_jaxpr/ppermute | solution.py:13
  286.5 10.2 %collective-permute-start = (f32[9,2048]{1,0:T(8,128)S(1)}, f32[9,2048]{1,0:T(8,128)S(1)}, u32[]{:S(2)}, u32[]{:S(2)}) collective-permute-start(f32[9,2048]{1,0:T(8,128)S(1)} %get-tuple-element.153), channel_id=1, source_target_pairs={{0,16},{16,32},{32,48},{48,64},{64,80},{80,96},{96,112},{112,128},... | collective-permute-start | bytes 221192 | tf_op jit(solution)/shard_map/while/body/eval_jaxpr/ppermute | solution.py:13
  288.5 11.6 %collective-permute-start.1 = (f32[32,2048]{1,0:T(8,128)S(1)}, f32[32,2048]{1,0:T(8,128)S(1)}, u32[]{:S(2)}, u32[]{:S(2)}) collective-permute-start(f32[32,2048]{1,0:T(8,128)S(1)} %get-tuple-element.154), channel_id=1, source_target_pairs={{0,16},{16,32},{32,48},{48,64},{64,80},{80,96},{96,112},{112,128},... | collective-permute-start | bytes 786440 | tf_op jit(solution)/shard_map/while/body/eval_jaxpr/ppermute | solution.py:13
  302.6 10.2 %collective-permute-start = (f32[9,2048]{1,0:T(8,128)S(1)}, f32[9,2048]{1,0:T(8,128)S(1)}, u32[]{:S(2)}, u32[]{:S(2)}) collective-permute-start(f32[9,2048]{1,0:T(8,128)S(1)} %get-tuple-element.153), channel_id=1, source_target_pairs={{0,16},{16,32},{32,48},{48,64},{64,80},{80,96},{96,112},{112,128},... | collective-permute-start | bytes 221192 | tf_op jit(solution)/shard_map/while/body/eval_jaxpr/ppermute | solution.py:13
  304.6 11.6 %collective-permute-start.1 = (f32[32,2048]{1,0:T(8,128)S(1)}, f32[32,2048]{1,0:T(8,128)S(1)}, u32[]{:S(2)}, u32[]{:S(2)}) collective-permute-start(f32[32,2048]{1,0:T(8,128)S(1)} %get-tuple-element.154), channel_id=1, source_target_pairs={{0,16},{16,32},{32,48},{48,64},{64,80},{80,96},{96,112},{112,128},... | collective-permute-start | bytes 786440 | tf_op jit(solution)/shard_map/while/body/eval_jaxpr/ppermute | solution.py:13
  318.7 10.2 %collective-permute-start = (f32[9,2048]{1,0:T(8,128)S(1)}, f32[9,2048]{1,0:T(8,128)S(1)}, u32[]{:S(2)}, u32[]{:S(2)}) collective-permute-start(f32[9,2048]{1,0:T(8,128)S(1)} %get-tuple-element.153), channel_id=1, source_target_pairs={{0,16},{16,32},{32,48},{48,64},{64,80},{80,96},{96,112},{112,128},... | collective-permute-start | bytes 221192 | tf_op jit(solution)/shard_map/while/body/eval_jaxpr/ppermute | solution.py:13
  320.7 11.6 %collective-permute-start.1 = (f32[32,2048]{1,0:T(8,128)S(1)}, f32[32,2048]{1,0:T(8,128)S(1)}, u32[]{:S(2)}, u32[]{:S(2)}) collective-permute-start(f32[32,2048]{1,0:T(8,128)S(1)} %get-tuple-element.154), channel_id=1, source_target_pairs={{0,16},{16,32},{32,48},{48,64},{64,80},{80,96},{96,112},{112,128},... | collective-permute-start | bytes 786440 | tf_op jit(solution)/shard_map/while/body/eval_jaxpr/ppermute | solution.py:13
  334.9 10.2 %collective-permute-start = (f32[9,2048]{1,0:T(8,128)S(1)}, f32[9,2048]{1,0:T(8,128)S(1)}, u32[]{:S(2)}, u32[]{:S(2)}) collective-permute-start(f32[9,2048]{1,0:T(8,128)S(1)} %get-tuple-element.153), channel_id=1, source_target_pairs={{0,16},{16,32},{32,48},{48,64},{64,80},{80,96},{96,112},{112,128},... | collective-permute-start | bytes 221192 | tf_op jit(solution)/shard_map/while/body/eval_jaxpr/ppermute | solution.py:13
  336.8 11.6 %collective-permute-start.1 = (f32[32,2048]{1,0:T(8,128)S(1)}, f32[32,2048]{1,0:T(8,128)S(1)}, u32[]{:S(2)}, u32[]{:S(2)}) collective-permute-start(f32[32,2048]{1,0:T(8,128)S(1)} %get-tuple-element.154), channel_id=1, source_target_pairs={{0,16},{16,32},{32,48},{48,64},{64,80},{80,96},{96,112},{112,128},... | collective-permute-start | bytes 786440 | tf_op jit(solution)/shard_map/while/body/eval_jaxpr/ppermute | solution.py:13
  351.0 10.2 %collective-permute-start = (f32[9,2048]{1,0:T(8,128)S(1)}, f32[9,2048]{1,0:T(8,128)S(1)}, u32[]{:S(2)}, u32[]{:S(2)}) collective-permute-start(f32[9,2048]{1,0:T(8,128)S(1)} %get-tuple-element.153), channel_id=1, source_target_pairs={{0,16},{16,32},{32,48},{48,64},{64,80},{80,96},{96,112},{112,128},... | collective-permute-start | bytes 221192 | tf_op jit(solution)/shard_map/while/body/eval_jaxpr/ppermute | solution.py:13
  352.9 11.6 %collective-permute-start.1 = (f32[32,2048]{1,0:T(8,128)S(1)}, f32[32,2048]{1,0:T(8,128)S(1)}, u32[]{:S(2)}, u32[]{:S(2)}) collective-permute-start(f32[32,2048]{1,0:T(8,128)S(1)} %get-tuple-element.154), channel_id=1, source_target_pairs={{0,16},{16,32},{32,48},{48,64},{64,80},{80,96},{96,112},{112,128},... | collective-permute-start | bytes 786440 | tf_op jit(solution)/shard_map/while/body/eval_jaxpr/ppermute | solution.py:13
  367.1 10.2 %collective-permute-start = (f32[9,2048]{1,0:T(8,128)S(1)}, f32[9,2048]{1,0:T(8,128)S(1)}, u32[]{:S(2)}, u32[]{:S(2)}) collective-permute-start(f32[9,2048]{1,0:T(8,128)S(1)} %get-tuple-element.153), channel_id=1, source_target_pairs={{0,16},{16,32},{32,48},{48,64},{64,80},{80,96},{96,112},{112,128},... | collective-permute-start | bytes 221192 | tf_op jit(solution)/shard_map/while/body/eval_jaxpr/ppermute | solution.py:13
  369.0 11.6 %collective-permute-start.1 = (f32[32,2048]{1,0:T(8,128)S(1)}, f32[32,2048]{1,0:T(8,128)S(1)}, u32[]{:S(2)}, u32[]{:S(2)}) collective-permute-start(f32[32,2048]{1,0:T(8,128)S(1)} %get-tuple-element.154), channel_id=1, source_target_pairs={{0,16},{16,32},{32,48},{48,64},{64,80},{80,96},{96,112},{112,128},... | collective-permute-start | bytes 786440 | tf_op jit(solution)/shard_map/while/body/eval_jaxpr/ppermute | solution.py:13
  383.2 10.2 %collective-permute-start = (f32[9,2048]{1,0:T(8,128)S(1)}, f32[9,2048]{1,0:T(8,128)S(1)}, u32[]{:S(2)}, u32[]{:S(2)}) collective-permute-start(f32[9,2048]{1,0:T(8,128)S(1)} %get-tuple-element.153), channel_id=1, source_target_pairs={{0,16},{16,32},{32,48},{48,64},{64,80},{80,96},{96,112},{112,128},... | collective-permute-start | bytes 221192 | tf_op jit(solution)/shard_map/while/body/eval_jaxpr/ppermute | solution.py:13
  385.1 11.6 %collective-permute-start.1 = (f32[32,2048]{1,0:T(8,128)S(1)}, f32[32,2048]{1,0:T(8,128)S(1)}, u32[]{:S(2)}, u32[]{:S(2)}) collective-permute-start(f32[32,2048]{1,0:T(8,128)S(1)} %get-tuple-element.154), channel_id=1, source_target_pairs={{0,16},{16,32},{32,48},{48,64},{64,80},{80,96},{96,112},{112,128},... | collective-permute-start | bytes 786440 | tf_op jit(solution)/shard_map/while/body/eval_jaxpr/ppermute | solution.py:13
  399.3 10.2 %collective-permute-start = (f32[9,2048]{1,0:T(8,128)S(1)}, f32[9,2048]{1,0:T(8,128)S(1)}, u32[]{:S(2)}, u32[]{:S(2)}) collective-permute-start(f32[9,2048]{1,0:T(8,128)S(1)} %get-tuple-element.153), channel_id=1, source_target_pairs={{0,16},{16,32},{32,48},{48,64},{64,80},{80,96},{96,112},{112,128},... | collective-permute-start | bytes 221192 | tf_op jit(solution)/shard_map/while/body/eval_jaxpr/ppermute | solution.py:13
  401.2 11.6 %collective-permute-start.1 = (f32[32,2048]{1,0:T(8,128)S(1)}, f32[32,2048]{1,0:T(8,128)S(1)}, u32[]{:S(2)}, u32[]{:S(2)}) collective-permute-start(f32[32,2048]{1,0:T(8,128)S(1)} %get-tuple-element.154), channel_id=1, source_target_pairs={{0,16},{16,32},{32,48},{48,64},{64,80},{80,96},{96,112},{112,128},... | collective-permute-start | bytes 786440 | tf_op jit(solution)/shard_map/while/body/eval_jaxpr/ppermute | solution.py:13
  415.4 10.2 %collective-permute-start = (f32[9,2048]{1,0:T(8,128)S(1)}, f32[9,2048]{1,0:T(8,128)S(1)}, u32[]{:S(2)}, u32[]{:S(2)}) collective-permute-start(f32[9,2048]{1,0:T(8,128)S(1)} %get-tuple-element.153), channel_id=1, source_target_pairs={{0,16},{16,32},{32,48},{48,64},{64,80},{80,96},{96,112},{112,128},... | collective-permute-start | bytes 221192 | tf_op jit(solution)/shard_map/while/body/eval_jaxpr/ppermute | solution.py:13
  417.3 11.6 %collective-permute-start.1 = (f32[32,2048]{1,0:T(8,128)S(1)}, f32[32,2048]{1,0:T(8,128)S(1)}, u32[]{:S(2)}, u32[]{:S(2)}) collective-permute-start(f32[32,2048]{1,0:T(8,128)S(1)} %get-tuple-element.154), channel_id=1, source_target_pairs={{0,16},{16,32},{32,48},{48,64},{64,80},{80,96},{96,112},{112,128},... | collective-permute-start | bytes 786440 | tf_op jit(solution)/shard_map/while/body/eval_jaxpr/ppermute | solution.py:13
  431.5 10.2 %collective-permute-start = (f32[9,2048]{1,0:T(8,128)S(1)}, f32[9,2048]{1,0:T(8,128)S(1)}, u32[]{:S(2)}, u32[]{:S(2)}) collective-permute-start(f32[9,2048]{1,0:T(8,128)S(1)} %get-tuple-element.153), channel_id=1, source_target_pairs={{0,16},{16,32},{32,48},{48,64},{64,80},{80,96},{96,112},{112,128},... | collective-permute-start | bytes 221192 | tf_op jit(solution)/shard_map/while/body/eval_jaxpr/ppermute | solution.py:13
  433.4 11.6 %collective-permute-start.1 = (f32[32,2048]{1,0:T(8,128)S(1)}, f32[32,2048]{1,0:T(8,128)S(1)}, u32[]{:S(2)}, u32[]{:S(2)}) collective-permute-start(f32[32,2048]{1,0:T(8,128)S(1)} %get-tuple-element.154), channel_id=1, source_target_pairs={{0,16},{16,32},{32,48},{48,64},{64,80},{80,96},{96,112},{112,128},... | collective-permute-start | bytes 786440 | tf_op jit(solution)/shard_map/while/body/eval_jaxpr/ppermute | solution.py:13
  447.6 10.2 %collective-permute-start = (f32[9,2048]{1,0:T(8,128)S(1)}, f32[9,2048]{1,0:T(8,128)S(1)}, u32[]{:S(2)}, u32[]{:S(2)}) collective-permute-start(f32[9,2048]{1,0:T(8,128)S(1)} %get-tuple-element.153), channel_id=1, source_target_pairs={{0,16},{16,32},{32,48},{48,64},{64,80},{80,96},{96,112},{112,128},... | collective-permute-start | bytes 221192 | tf_op jit(solution)/shard_map/while/body/eval_jaxpr/ppermute | solution.py:13
  449.5 11.6 %collective-permute-start.1 = (f32[32,2048]{1,0:T(8,128)S(1)}, f32[32,2048]{1,0:T(8,128)S(1)}, u32[]{:S(2)}, u32[]{:S(2)}) collective-permute-start(f32[32,2048]{1,0:T(8,128)S(1)} %get-tuple-element.154), channel_id=1, source_target_pairs={{0,16},{16,32},{32,48},{48,64},{64,80},{80,96},{96,112},{112,128},... | collective-permute-start | bytes 786440 | tf_op jit(solution)/shard_map/while/body/eval_jaxpr/ppermute | solution.py:13
  463.7 10.2 %collective-permute-start = (f32[9,2048]{1,0:T(8,128)S(1)}, f32[9,2048]{1,0:T(8,128)S(1)}, u32[]{:S(2)}, u32[]{:S(2)}) collective-permute-start(f32[9,2048]{1,0:T(8,128)S(1)} %get-tuple-element.153), channel_id=1, source_target_pairs={{0,16},{16,32},{32,48},{48,64},{64,80},{80,96},{96,112},{112,128},... | collective-permute-start | bytes 221192 | tf_op jit(solution)/shard_map/while/body/eval_jaxpr/ppermute | solution.py:13
  465.6 11.6 %collective-permute-start.1 = (f32[32,2048]{1,0:T(8,128)S(1)}, f32[32,2048]{1,0:T(8,128)S(1)}, u32[]{:S(2)}, u32[]{:S(2)}) collective-permute-start(f32[32,2048]{1,0:T(8,128)S(1)} %get-tuple-element.154), channel_id=1, source_target_pairs={{0,16},{16,32},{32,48},{48,64},{64,80},{80,96},{96,112},{112,128},... | collective-permute-start | bytes 786440 | tf_op jit(solution)/shard_map/while/body/eval_jaxpr/ppermute | solution.py:13
  479.8 10.2 %collective-permute-start = (f32[9,2048]{1,0:T(8,128)S(1)}, f32[9,2048]{1,0:T(8,128)S(1)}, u32[]{:S(2)}, u32[]{:S(2)}) collective-permute-start(f32[9,2048]{1,0:T(8,128)S(1)} %get-tuple-element.153), channel_id=1, source_target_pairs={{0,16},{16,32},{32,48},{48,64},{64,80},{80,96},{96,112},{112,128},... | collective-permute-start | bytes 221192 | tf_op jit(solution)/shard_map/while/body/eval_jaxpr/ppermute | solution.py:13
  481.7 11.6 %collective-permute-start.1 = (f32[32,2048]{1,0:T(8,128)S(1)}, f32[32,2048]{1,0:T(8,128)S(1)}, u32[]{:S(2)}, u32[]{:S(2)}) collective-permute-start(f32[32,2048]{1,0:T(8,128)S(1)} %get-tuple-element.154), channel_id=1, source_target_pairs={{0,16},{16,32},{32,48},{48,64},{64,80},{80,96},{96,112},{112,128},... | collective-permute-start | bytes 786440 | tf_op jit(solution)/shard_map/while/body/eval_jaxpr/ppermute | solution.py:13
  495.9 10.2 %collective-permute-start = (f32[9,2048]{1,0:T(8,128)S(1)}, f32[9,2048]{1,0:T(8,128)S(1)}, u32[]{:S(2)}, u32[]{:S(2)}) collective-permute-start(f32[9,2048]{1,0:T(8,128)S(1)} %get-tuple-element.153), channel_id=1, source_target_pairs={{0,16},{16,32},{32,48},{48,64},{64,80},{80,96},{96,112},{112,128},... | collective-permute-start | bytes 221192 | tf_op jit(solution)/shard_map/while/body/eval_jaxpr/ppermute | solution.py:13
  497.8 11.6 %collective-permute-start.1 = (f32[32,2048]{1,0:T(8,128)S(1)}, f32[32,2048]{1,0:T(8,128)S(1)}, u32[]{:S(2)}, u32[]{:S(2)}) collective-permute-start(f32[32,2048]{1,0:T(8,128)S(1)} %get-tuple-element.154), channel_id=1, source_target_pairs={{0,16},{16,32},{32,48},{48,64},{64,80},{80,96},{96,112},{112,128},... | collective-permute-start | bytes 786440 | tf_op jit(solution)/shard_map/while/body/eval_jaxpr/ppermute | solution.py:13
  512.0 10.2 %collective-permute-start = (f32[9,2048]{1,0:T(8,128)S(1)}, f32[9,2048]{1,0:T(8,128)S(1)}, u32[]{:S(2)}, u32[]{:S(2)}) collective-permute-start(f32[9,2048]{1,0:T(8,128)S(1)} %get-tuple-element.153), channel_id=1, source_target_pairs={{0,16},{16,32},{32,48},{48,64},{64,80},{80,96},{96,112},{112,128},... | collective-permute-start | bytes 221192 | tf_op jit(solution)/shard_map/while/body/eval_jaxpr/ppermute | solution.py:13
  513.9 11.6 %collective-permute-start.1 = (f32[32,2048]{1,0:T(8,128)S(1)}, f32[32,2048]{1,0:T(8,128)S(1)}, u32[]{:S(2)}, u32[]{:S(2)}) collective-permute-start(f32[32,2048]{1,0:T(8,128)S(1)} %get-tuple-element.154), channel_id=1, source_target_pairs={{0,16},{16,32},{32,48},{48,64},{64,80},{80,96},{96,112},{112,128},... | collective-permute-start | bytes 786440 | tf_op jit(solution)/shard_map/while/body/eval_jaxpr/ppermute | solution.py:13
  528.1 10.2 %collective-permute-start = (f32[9,2048]{1,0:T(8,128)S(1)}, f32[9,2048]{1,0:T(8,128)S(1)}, u32[]{:S(2)}, u32[]{:S(2)}) collective-permute-start(f32[9,2048]{1,0:T(8,128)S(1)} %get-tuple-element.153), channel_id=1, source_target_pairs={{0,16},{16,32},{32,48},{48,64},{64,80},{80,96},{96,112},{112,128},... | collective-permute-start | bytes 221192 | tf_op jit(solution)/shard_map/while/body/eval_jaxpr/ppermute | solution.py:13
  530.1 11.6 %collective-permute-start.1 = (f32[32,2048]{1,0:T(8,128)S(1)}, f32[32,2048]{1,0:T(8,128)S(1)}, u32[]{:S(2)}, u32[]{:S(2)}) collective-permute-start(f32[32,2048]{1,0:T(8,128)S(1)} %get-tuple-element.154), channel_id=1, source_target_pairs={{0,16},{16,32},{32,48},{48,64},{64,80},{80,96},{96,112},{112,128},... | collective-permute-start | bytes 786440 | tf_op jit(solution)/shard_map/while/body/eval_jaxpr/ppermute | solution.py:13
  544.2 10.2 %collective-permute-start = (f32[9,2048]{1,0:T(8,128)S(1)}, f32[9,2048]{1,0:T(8,128)S(1)}, u32[]{:S(2)}, u32[]{:S(2)}) collective-permute-start(f32[9,2048]{1,0:T(8,128)S(1)} %get-tuple-element.153), channel_id=1, source_target_pairs={{0,16},{16,32},{32,48},{48,64},{64,80},{80,96},{96,112},{112,128},... | collective-permute-start | bytes 221192 | tf_op jit(solution)/shard_map/while/body/eval_jaxpr/ppermute | solution.py:13
  546.2 11.6 %collective-permute-start.1 = (f32[32,2048]{1,0:T(8,128)S(1)}, f32[32,2048]{1,0:T(8,128)S(1)}, u32[]{:S(2)}, u32[]{:S(2)}) collective-permute-start(f32[32,2048]{1,0:T(8,128)S(1)} %get-tuple-element.154), channel_id=1, source_target_pairs={{0,16},{16,32},{32,48},{48,64},{64,80},{80,96},{96,112},{112,128},... | collective-permute-start | bytes 786440 | tf_op jit(solution)/shard_map/while/body/eval_jaxpr/ppermute | solution.py:13
  560.3 10.2 %collective-permute-start = (f32[9,2048]{1,0:T(8,128)S(1)}, f32[9,2048]{1,0:T(8,128)S(1)}, u32[]{:S(2)}, u32[]{:S(2)}) collective-permute-start(f32[9,2048]{1,0:T(8,128)S(1)} %get-tuple-element.153), channel_id=1, source_target_pairs={{0,16},{16,32},{32,48},{48,64},{64,80},{80,96},{96,112},{112,128},... | collective-permute-start | bytes 221192 | tf_op jit(solution)/shard_map/while/body/eval_jaxpr/ppermute | solution.py:13
  562.3 11.6 %collective-permute-start.1 = (f32[32,2048]{1,0:T(8,128)S(1)}, f32[32,2048]{1,0:T(8,128)S(1)}, u32[]{:S(2)}, u32[]{:S(2)}) collective-permute-start(f32[32,2048]{1,0:T(8,128)S(1)} %get-tuple-element.154), channel_id=1, source_target_pairs={{0,16},{16,32},{32,48},{48,64},{64,80},{80,96},{96,112},{112,128},... | collective-permute-start | bytes 786440 | tf_op jit(solution)/shard_map/while/body/eval_jaxpr/ppermute | solution.py:13
  576.4 10.2 %collective-permute-start = (f32[9,2048]{1,0:T(8,128)S(1)}, f32[9,2048]{1,0:T(8,128)S(1)}, u32[]{:S(2)}, u32[]{:S(2)}) collective-permute-start(f32[9,2048]{1,0:T(8,128)S(1)} %get-tuple-element.153), channel_id=1, source_target_pairs={{0,16},{16,32},{32,48},{48,64},{64,80},{80,96},{96,112},{112,128},... | collective-permute-start | bytes 221192 | tf_op jit(solution)/shard_map/while/body/eval_jaxpr/ppermute | solution.py:13
  578.4 11.6 %collective-permute-start.1 = (f32[32,2048]{1,0:T(8,128)S(1)}, f32[32,2048]{1,0:T(8,128)S(1)}, u32[]{:S(2)}, u32[]{:S(2)}) collective-permute-start(f32[32,2048]{1,0:T(8,128)S(1)} %get-tuple-element.154), channel_id=1, source_target_pairs={{0,16},{16,32},{32,48},{48,64},{64,80},{80,96},{96,112},{112,128},... | collective-permute-start | bytes 786440 | tf_op jit(solution)/shard_map/while/body/eval_jaxpr/ppermute | solution.py:13
  592.5 10.2 %collective-permute-start = (f32[9,2048]{1,0:T(8,128)S(1)}, f32[9,2048]{1,0:T(8,128)S(1)}, u32[]{:S(2)}, u32[]{:S(2)}) collective-permute-start(f32[9,2048]{1,0:T(8,128)S(1)} %get-tuple-element.153), channel_id=1, source_target_pairs={{0,16},{16,32},{32,48},{48,64},{64,80},{80,96},{96,112},{112,128},... | collective-permute-start | bytes 221192 | tf_op jit(solution)/shard_map/while/body/eval_jaxpr/ppermute | solution.py:13
  594.5 11.6 %collective-permute-start.1 = (f32[32,2048]{1,0:T(8,128)S(1)}, f32[32,2048]{1,0:T(8,128)S(1)}, u32[]{:S(2)}, u32[]{:S(2)}) collective-permute-start(f32[32,2048]{1,0:T(8,128)S(1)} %get-tuple-element.154), channel_id=1, source_target_pairs={{0,16},{16,32},{32,48},{48,64},{64,80},{80,96},{96,112},{112,128},... | collective-permute-start | bytes 786440 | tf_op jit(solution)/shard_map/while/body/eval_jaxpr/ppermute | solution.py:13
where the time goes:
time: 612 us; the launch traced here: 610 us
  waiting for transfers between devices  297 us (49%)
  starting transfers between devices  120 us (20%)
  blocking collectives  105 us (17%)
  matrix products  81.1 us (13%)
    ppermute x62, waiting for transfers between devices, from_behind(): lax.ppermute(shard, axis, [(i, (i + by) % size) for i in range(size)])  297 us
    ppermute x62, starting transfers between devices, from_behind(): lax.ppermute(shard, axis, [(i, (i + by) % size) for i in range(size)])  120 us
    dot_general x32, matrix products, apply_tile(): jnp.einsum('cg,pg->cp', far_probes, tile, preferred_element_type=jnp.floa...  81.1 us
    all_gather x1, blocking collectives, body(): lax.all_gather(scaled, 'grp', axis=1, tiled=True)  53.4 us
    all_gather x1, blocking collectives, body(): lax.all_gather(probes, 'grp', axis=1, tiled=True)  51.8 us
  transfers between devices with their start and end apart: 62, of which 62 were waited for; matrix products, arithmetic and copies ran while one was open for 0% of the time, Pallas kernels for 0%

commit v1 on v0

v1 whole, which is shorter than its diff:
```python
import functools
import math

import jax
import jax.numpy as jnp
from jax import lax
from jax.experimental import pallas as pl
from jax.experimental.pallas import tpu as pltpu
from jax.sharding import Mesh, PartitionSpec as P

AXES = ("x", "zl", "c", "y", "zh")
COL_AXES = ("zl", "zh")
ROW_AXES = ("x", "y")
LANES = 128
UNIT = 16
DEPTH = 128
TILE = 256
STEP = 32
SCALE = math.sqrt(5.0) / 3.0
RATE = -3.0 / math.log(2.0)
TINY = 1e-30
PREPARE_LIMIT = 60 * 1024 * 1024
LIMIT = 32 * 1024 * 1024
WHOLE = pl.BlockSpec(memory_space=pltpu.VMEM)


def extended(x, norm, one, ref):
    dims = x.shape[0]
    ref[...] = jnp.zeros(ref.shape, jnp.float32)
    ref[0:dims] = x
    ref[dims : dims + 1] = norm
    ref[dims + 1 : dims + 2] = one


def prepare_kernel(points_ref, length_ref, probes_ref, row_ref, cols_ref):
    dims, n_probes = points_ref.shape[0], probes_ref.shape[0]
    at = lax.broadcasted_iota(jnp.int32, (dims, dims), 0) == lax.broadcasted_iota(jnp.int32, (dims, dims), 1)
    length = jnp.sum(jnp.where(at, length_ref[...], 0.0), axis=1, keepdims=True)
    x = points_ref[...] * (length * SCALE)
    norm = jnp.sum(x * x, axis=0, keepdims=True)
    extended(x, norm, jnp.ones_like(norm), row_ref)
    probes = probes_ref[...]
    for start in range(0, cols_ref.shape[0], dims + n_probes):
        cols_ref[start : start + dims] = x
        cols_ref[start + dims : start + dims + n_probes] = probes


def split3(value):
    first = value.astype(jnp.bfloat16)
    rest = value - first.astype(jnp.float32)
    second = rest.astype(jnp.bfloat16)
    third = (rest - second.astype(jnp.float32)).astype(jnp.bfloat16)
    return first, second, third


def halves(squared):
    squared = jnp.maximum(squared, TINY)
    v = squared * lax.rsqrt(squared)
    k = ((squared + v) + (1.0 / 3.0)) * jnp.exp2(v * RATE)
    high = k.astype(jnp.bfloat16)
    return high, (k - high.astype(jnp.float32)).astype(jnp.bfloat16)


def block_kernel(last, dims, *refs):
    if last:
        a, cols_ref, sum_ref, out_ref, b, q, unit, d0, d1, h0, h1, acc = refs
        n_probes = out_ref.shape[1]
    else:
        rows_ref, cols_ref, acc, a, b, q, unit, d0, d1, h0, h1 = refs
        n_probes = acc.shape[1] // 2
    d, h = (d0, d1), (h0, h1)
    per = dims + n_probes
    n_rows, n_cols = a.shape[0] * TILE // LANES, cols_ref.shape[0] // per
    each = TILE // LANES
    zero = jnp.zeros((UNIT, LANES), jnp.bfloat16)

    if not last:
        for s in range(n_rows):
            u1, u2, u3 = split3(rows_ref[s])
            lanes = slice((s % each) * LANES, (s % each + 1) * LANES)
            a[s // each, :, lanes] = jnp.concatenate([u1, u1, u2, u2, u1, u3, zero, zero], axis=0)
    for s in range(n_cols):
        x = cols_ref[s * per : s * per + dims]
        norm = jnp.sum(x * x, axis=0, keepdims=True)
        extended(-2.0 * x, jnp.ones_like(norm), norm, unit.at[s])
        v1, v2, v3 = split3(unit[s])
        lanes = slice((s % each) * LANES, (s % each + 1) * LANES)
        stack = jnp.concatenate([v1, v2, v1, v2, v3, v1, zero, zero], axis=0)
        b[s // each, lanes, :] = stack.T
        p = cols_ref[s * per + dims : (s + 1) * per]
        p1 = p.astype(jnp.bfloat16)
        p2 = (p - p1.astype(jnp.float32)).astype(jnp.bfloat16)
        both = jnp.concatenate([p1, p2], axis=0)
        q[s // each, :, lanes] = both
        q[s // each, :, lanes.start + TILE : lanes.stop + TILE] = both
    acc[...] = sum_ref[...] if last else jnp.zeros_like(acc)
    tiles, chunks = a.shape[0], b.shape[0]

    chain = 4 if last else 2

    def strip(i, carry):
        for at in range(chain * tiles):
            chunk, tile = i * chain + at // tiles, at % tiles
            now, then = at % 2, 1 - at % 2
            before = chunk if tile > 0 else jnp.maximum(chunk - 1, 0)
            after = chunk if tile + 1 < tiles else jnp.minimum(chunk + 1, chunks - 1)
            product = jnp.dot(q[before], h[then][...], preferred_element_type=jnp.float32)
            ahead = jnp.dot(b[after], a[(tile + 1) % tiles], preferred_element_type=jnp.float32)
            acc[(tile - 1) % tiles] += product
            d[then][...] = ahead
            for start in range(0, TILE, STEP):
                high, low = halves(d[now][start : start + STEP])
                h[now][start : start + STEP] = high
                h[now][TILE + start : TILE + start + STEP] = low
        return carry

    h1[...] = jnp.zeros_like(h1)
    d0[...] = jnp.dot(b[0], a[0], preferred_element_type=jnp.float32)
    lax.fori_loop(0, chunks // chain, strip, 0)
    acc[tiles - 1] += jnp.dot(q[chunks - 1], h[(tiles - 1) % 2][...], preferred_element_type=jnp.float32)
    if not last:
        return
    for s in range(n_rows):
        lanes = slice((s % each) * LANES, (s % each + 1) * LANES)
        out_ref[s] = 3.0 * (acc[s // each, 0:n_probes, lanes] + acc[s // each, n_probes:, lanes])


def block(rows, cols, dims, n_probes, total=None):
    f32, bf16 = jnp.float32, jnp.bfloat16
    last = total is not None
    n_rows = rows.shape[0] * TILE // LANES if last else rows.shape[0]
    n_cols = cols.shape[0] // (dims + n_probes)
    row_tiles, col_tiles = n_rows * LANES // TILE, n_cols * LANES // TILE
    sums = jax.ShapeDtypeStruct((row_tiles, 2 * n_probes, TILE), f32)
    turned = jax.ShapeDtypeStruct((row_tiles, DEPTH, TILE), bf16)
    entries = n_rows * n_cols * LANES * LANES
    return pl.pallas_call(
        functools.partial(block_kernel, last, dims),
        out_shape=jax.ShapeDtypeStruct((n_rows, n_probes, LANES), f32) if last else (sums, turned),
        in_specs=[WHOLE] * (3 if last else 2),
        out_specs=WHOLE if last else (WHOLE, WHOLE),
        scratch_shapes=[
            pltpu.VMEM((col_tiles, TILE, DEPTH), bf16),
            pltpu.VMEM((col_tiles, 2 * n_probes, 2 * TILE), bf16),
            pltpu.VMEM((n_cols, UNIT, LANES), f32),
            pltpu.VMEM((TILE, TILE), f32),
            pltpu.VMEM((TILE, TILE), f32),
            pltpu.VMEM((2 * TILE, TILE), bf16),
            pltpu.VMEM((2 * TILE, TILE), bf16),
        ]
        + [pltpu.VMEM(sums.shape, f32)] * last,
        compiler_params=pltpu.CompilerParams(vmem_limit_bytes=LIMIT),
        cost_estimate=pl.CostEstimate(flops=entries * 2000, bytes_accessed=4 * cols.size, transcendentals=2 * entries),
        name="block_last" if last else "block_first",
    )(*((rows, cols, total) if last else (rows, cols)))


def body(points, inv_length, probes, noise):
    n_cols = lax.axis_size(COL_AXES)
    (dims, width), n_probes = points.shape, probes.shape[0]
    per = dims + n_probes
    f32 = jnp.float32
    row, cols = pl.pallas_call(
        prepare_kernel,
        out_shape=(
            jax.ShapeDtypeStruct((UNIT, width), f32),
            jax.ShapeDtypeStruct((n_cols * per, width), f32),
        ),
        in_specs=[WHOLE] * 3,
        out_specs=(WHOLE, WHOLE),
        compiler_params=pltpu.CompilerParams(vmem_limit_bytes=PREPARE_LIMIT),
        name="prepare",
    )(points, inv_length[None, :], probes)
    cols = lax.all_to_all(cols.reshape(n_cols * per, 1, width), COL_AXES, 0, 0, tiled=True).reshape(n_cols * per, width)
    other = lax.ppermute(cols, "c", [(0, 1), (1, 0)])
    rows = lax.all_gather(row, ROW_AXES, axis=0)
    total, turned = block(rows, cols, dims, n_probes)
    part = block(turned, other, dims, n_probes, total)
    part = lax.all_to_all(part, ROW_AXES, 0, 0, tiled=True)
    return jnp.sum(part, axis=0) + noise[0] * probes


def solution(mesh):
    fine = Mesh(mesh.devices.reshape(4, 4, 2, 4, 4), AXES)
    split = P(None, AXES)
    return jax.shard_map(body, mesh=fine, in_specs=(split, P(), split, P()), out_specs=split, check_vma=False)
```

time: 612 us -> 75.7 us (0.12)
  the two profiles are of different devices: /device:TPU:128 before, /device:TPU:64 now
where the time goes in v1:
time: 75.7 us; the launch traced here: 75.3 us
  blocking collectives  24 us (32%)
  starting transfers between devices  23 us (30%)
  Pallas kernels  18.5 us (24%)
  waiting for transfers between devices  8.52 us (11%)
    all_gather x1, blocking collectives, body(): rows = lax.all_gather(row, ROW_AXES, axis=0)  24 us
    pallas_call x2, Pallas kernels, block(): pl.pallas_call(functools.partial(block_kernel, last, dims), out_shape=jax...  16.9 us
    all_to_all x1, starting transfers between devices, body(): lax.all_to_all(cols.reshape(n_cols * per, 1, width), COL_AXES, 0, 0, tile...  14.9 us
    all_to_all x1, waiting for transfers between devices, body(): part = lax.all_to_all(part, ROW_AXES, 0, 0, tiled=True)  8.51 us
    all_to_all x1, starting transfers between devices, body(): part = lax.all_to_all(part, ROW_AXES, 0, 0, tiled=True)  6.16 us
    ppermute x1, starting transfers between devices, body(): other = lax.ppermute(cols, 'c', [(0, 1), (1, 0)])  1.92 us
    pallas_call x1, Pallas kernels, body(): pl.pallas_call(prepare_kernel, out_shape=(jax.ShapeDtypeStruct((UNIT, wid...  1.58 us
  transfers between devices with their start and end apart: 3, of which 1 were waited for; matrix products, arithmetic and copies ran while one was open for 0% of the time, Pallas kernels for 11%

profile of v1, /device:TPU:64, one launch (start us, length us, event | category | flops | bytes accessed | tf_op | source)
XLA Modules:
  0.0 75.3 jit_solution(16190709378122724337)
XLA Ops:
  0.0 1.6 %prepare.1 = (f32[16,128]{1,0:T(8,128)}, f32[656,128]{1,0:T(8,128)}) custom-call(f32[9,128]{1,0:T(8,128)} %points_ref.1, f32[1,9]{1,0:T(1,128)} %bitcast.12, f32[32,128]{1,0:T(8,128)} %probes_ref.1), custom_call_target="tpu_custom_call" | custom-call | tf_op jit(solution)/shard_map/prepare/pallas_call | solution.py:163
  1.6 0.0 copy-start.1
  1.6 14.9 %all-to-all-start = ((f32[656,1,128]{2,1,0:T(1,128)}), f32[656,1,128]{2,1,0:T(1,128)S(1)}, u32[]{:S(2)}, u32[]{:S(2)}) async-start(f32[656,1,128]{2,1,0:T(1,128)} %bitcast.11), calls=%async_computation | async-start | bytes 671744 | tf_op jit(solution)/shard_map/all_to_all | solution.py:174
  16.5 0.0 copy-done.1
  16.5 24.0 %all-gather = f32[256,128]{1,0:T(8,128)S(1)} all-gather(f32[16,128]{1,0:T(8,128)S(1)} %copy-done.1), channel_id=2, replica_groups=mesh['x'=4,'zl'=4,'c'=2,'y'=4,'zh'=4] {'x','y'}, dimensions={0}, use_global_device_ids=true | all-gather | bytes 139264 | tf_op jit(solution)/shard_map/all_gather | solution.py:176
  40.4 0.0 all-to-all-done
  40.4 1.9 %collective-permute-start = (f32[656,128]{1,0:T(8,128)S(1)}, f32[656,128]{1,0:T(8,128)S(1)}, u32[]{:S(2)}, u32[]{:S(2)}) collective-permute-start(f32[656,128]{1,0:T(8,128)S(1)} %bitcast.8), channel_id=1, source_target_pairs={{0,16},{16,0},{1,17},{17,1},{2,18},{18,2},{3,19},{19,3},{4,20},{20... | collective-permute-start | bytes 1007624 | tf_op jit(solution)/shard_map/ppermute | solution.py:175
  42.4 8.2 %block_first.1 = (f32[8,64,256]{2,1,0:T(8,128)S(1)}, bf16[8,128,256]{2,1,0:T(8,128)(2,1)S(1)}) custom-call(f32[16,16,128]{2,1,0:T(8,128)S(1)} %bitcast.10, f32[656,128]{1,0:T(8,128)S(1)} %bitcast.9), custom_call_target="tpu_custom_call" | custom-call | flops 8388608000 | bytes 335872 | tf_op jit(solution)/shard_map/block_first/pallas_call | solution.py:137
  50.5 0.0 collective-permute-done.refs_1_
  50.5 8.7 %block_last.1 = f32[16,32,128]{2,1,0:T(8,128)} custom-call(bf16[8,128,256]{2,1,0:T(8,128)(2,1)S(1)} %get-tuple-element.11.refs_0_, f32[656,128]{1,0:T(8,128)S(1)} %collective-permute-done.refs_1_, f32[8,64,256]{2,1,0:T(8,128)S(1)} %get-tuple-element.12.refs_2_), custom_call_target="tpu_custom_call" | custom-call | flops 8388608000 | bytes 335872 | tf_op jit(solution)/shard_map/block_last/pallas_call | solution.py:137
  59.3 6.2 %all-to-all-start.1 = ((f32[16,32,128]{2,1,0:T(8,128)}), f32[16,32,128]{2,1,0:T(8,128)S(1)}, u32[]{:S(2)}, u32[]{:S(2)}) async-start(f32[16,32,128]{2,1,0:T(8,128)} %block_last.1), calls=%async_computation.1 | async-start | bytes 524288 | tf_op jit(solution)/shard_map/all_to_all | solution.py:179
  66.1 0.0 copy-start
  66.1 8.5 %all-to-all-done.1 = f32[16,32,128]{2,1,0:T(8,128)S(1)} async-done(((f32[16,32,128]{2,1,0:T(8,128)}), f32[16,32,128]{2,1,0:T(8,128)S(1)}, u32[]{:S(2)}, u32[]{:S(2)}) %all-to-all-start.1) | async-done | bytes 262176 | tf_op jit(solution)/shard_map/all_to_all | solution.py:179
  74.6 0.0 copy-done
  74.6 0.6 multiply_add_fusion
  (1 shorter events, 0.0 us)
Async XLA Ops:
  1.6 14.9 %copy-start.1 = (f32[16,128]{1,0:T(8,128)S(1)}, f32[16,128]{1,0:T(8,128)}, u32[]{:S(2)}) copy-start(f32[16,128]{1,0:T(8,128)} %get-tuple-element.9) | copy-start | bytes 24580
  1.6 38.9 %all-to-all-start = ((f32[656,1,128]{2,1,0:T(1,128)}), f32[656,1,128]{2,1,0:T(1,128)S(1)}, u32[]{:S(2)}, u32[]{:S(2)}) async-start(f32[656,1,128]{2,1,0:T(1,128)} %bitcast.11), calls=%async_computation | async-start | bytes 671744 | tf_op jit(solution)/shard_map/all_to_all | solution.py:174
  40.4 10.1 %collective-permute-start = (f32[656,128]{1,0:T(8,128)S(1)}, f32[656,128]{1,0:T(8,128)S(1)}, u32[]{:S(2)}, u32[]{:S(2)}) collective-permute-start(f32[656,128]{1,0:T(8,128)S(1)} %bitcast.8), channel_id=1, source_target_pairs={{0,16},{16,0},{1,17},{17,1},{2,18},{18,2},{3,19},{19,3},{4,20},{20... | collective-permute-start | bytes 1007624 | tf_op jit(solution)/shard_map/ppermute | solution.py:175
  59.3 15.3 %all-to-all-start.1 = ((f32[16,32,128]{2,1,0:T(8,128)}), f32[16,32,128]{2,1,0:T(8,128)S(1)}, u32[]{:S(2)}, u32[]{:S(2)}) async-start(f32[16,32,128]{2,1,0:T(8,128)} %block_last.1), calls=%async_computation.1 | async-start | bytes 524288 | tf_op jit(solution)/shard_map/all_to_all | solution.py:179
  66.1 8.5 %copy-start = (f32[32,128]{1,0:T(8,128)S(1)}, f32[32,128]{1,0:T(8,128)}, u32[]{:S(2)}) copy-start(f32[32,128]{1,0:T(8,128)} %probes_ref.1) | copy-start | bytes 49156

commit v2 on v1

--- a/solution.py
+++ b/solution.py
@@ -93,36 +93,40 @@
         both = jnp.concatenate([p1, p2], axis=0)
         q[s // each, :, lanes] = both
         q[s // each, :, lanes.start + TILE : lanes.stop + TILE] = both
-    acc[...] = sum_ref[...] if last else jnp.zeros_like(acc)
     tiles, chunks = a.shape[0], b.shape[0]
+    count = tiles * chunks
 
-    chain = 4 if last else 2
+    def distance(at):
+        return jnp.dot(b[at // tiles], a[at % tiles], preferred_element_type=jnp.float32)
 
-    def strip(i, carry):
-        for at in range(chain * tiles):
-            chunk, tile = i * chain + at // tiles, at % tiles
-            now, then = at % 2, 1 - at % 2
-            before = chunk if tile > 0 else jnp.maximum(chunk - 1, 0)
-            after = chunk if tile + 1 < tiles else jnp.minimum(chunk + 1, chunks - 1)
-            product = jnp.dot(q[before], h[then][...], preferred_element_type=jnp.float32)
-            ahead = jnp.dot(b[after], a[(tile + 1) % tiles], preferred_element_type=jnp.float32)
-            acc[(tile - 1) % tiles] += product
-            d[then][...] = ahead
-            for start in range(0, TILE, STEP):
-                high, low = halves(d[now][start : start + STEP])
-                h[now][start : start + STEP] = high
-                h[now][TILE + start : TILE + start + STEP] = low
-        return carry
+    def product(at):
+        return jnp.dot(q[at // tiles], h[at % 2][...], preferred_element_type=jnp.float32)
 
-    h1[...] = jnp.zeros_like(h1)
-    d0[...] = jnp.dot(b[0], a[0], preferred_element_type=jnp.float32)
-    lax.fori_loop(0, chunks // chain, strip, 0)
-    acc[tiles - 1] += jnp.dot(q[chunks - 1], h[(tiles - 1) % 2][...], preferred_element_type=jnp.float32)
-    if not last:
-        return
-    for s in range(n_rows):
-        lanes = slice((s % each) * LANES, (s % each + 1) * LANES)
-        out_ref[s] = 3.0 * (acc[s // each, 0:n_probes, lanes] + acc[s // each, n_probes:, lanes])
+    def add(at, value):
+        tile = at % tiles
+        if at >= tiles:
+            value = acc[tile] + value
+        elif last:
+            value = sum_ref[tile] + value
+        if not last or at < count - tiles:
+            acc[tile] = value
+            return
+        value = 3.0 * (value[0:n_probes] + value[n_probes:])
+        for s in range(each):
+            out_ref[tile * each + s] = value[:, s * LANES : (s + 1) * LANES]
+
+    d0[...] = distance(0)
+    for at in range(count):
+        now, then = at % 2, 1 - at % 2
+        if at > 0:
+            add(at - 1, product(at - 1))
+        if at + 1 < count:
+            d[then][...] = distance(at + 1)
+        for start in range(0, TILE, STEP):
+            high, low = halves(d[now][start : start + STEP])
+            h[now][start : start + STEP] = high
+            h[now][TILE + start : TILE + start + STEP] = low
+    add(count - 1, product(count - 1))
 
 
 def block(rows, cols, dims, n_probes, total=None):

time: 75.7 us -> 74.8 us (0.988)
  Pallas kernels: 18.5 us -> 17.6 us
    pallas_call x2, Pallas kernels: 16.9 us -> 16 us  [block(): pl.pallas_call(functools.partial(block_kernel, last, dims), out_shape=jax...]
  transfers between devices with their start and end apart: 3 -> 3, of which waited for: 1 -> 1; matrix products, arithmetic and copies ran while one was open for 0% -> 0% of each run, Pallas kernels for 11% -> 10%
where the time goes in v2:
time: 74.8 us; the launch traced here: 74.4 us
  blocking collectives  24 us (32%)
  starting transfers between devices  23 us (31%)
  Pallas kernels  17.6 us (24%)
  waiting for transfers between devices  8.5 us (11%)
    all_gather x1, blocking collectives, body(): rows = lax.all_gather(row, ROW_AXES, axis=0)  24 us
    pallas_call x2, Pallas kernels, block(): pl.pallas_call(functools.partial(block_kernel, last, dims), out_shape=jax...  16 us
    all_to_all x1, starting transfers between devices, body(): lax.all_to_all(cols.reshape(n_cols * per, 1, width), COL_AXES, 0, 0, tile...  14.9 us
    all_to_all x1, waiting for transfers between devices, body(): part = lax.all_to_all(part, ROW_AXES, 0, 0, tiled=True)  8.49 us
    all_to_all x1, starting transfers between devices, body(): part = lax.all_to_all(part, ROW_AXES, 0, 0, tiled=True)  6.17 us
    ppermute x1, starting transfers between devices, body(): other = lax.ppermute(cols, 'c', [(0, 1), (1, 0)])  1.92 us
    pallas_call x1, Pallas kernels, body(): pl.pallas_call(prepare_kernel, out_shape=(jax.ShapeDtypeStruct((UNIT, wid...  1.58 us
  transfers between devices with their start and end apart: 3, of which 1 were waited for; matrix products, arithmetic and copies ran while one was open for 0% of the time, Pallas kernels for 10%

profile of v2, /device:TPU:64, one launch (start us, length us, event | category | flops | bytes accessed | tf_op | source)
XLA Modules:
  0.0 74.4 jit_solution(1763708662024346948)
XLA Ops:
  0.0 1.6 %prepare.1 = (f32[16,128]{1,0:T(8,128)}, f32[656,128]{1,0:T(8,128)}) custom-call(f32[9,128]{1,0:T(8,128)} %points_ref.1, f32[1,9]{1,0:T(1,128)} %bitcast.12, f32[32,128]{1,0:T(8,128)} %probes_ref.1), custom_call_target="tpu_custom_call" | custom-call | tf_op jit(solution)/shard_map/prepare/pallas_call | solution.py:167
  1.6 0.0 copy-start.1
  1.6 14.9 %all-to-all-start = ((f32[656,1,128]{2,1,0:T(1,128)}), f32[656,1,128]{2,1,0:T(1,128)S(1)}, u32[]{:S(2)}, u32[]{:S(2)}) async-start(f32[656,1,128]{2,1,0:T(1,128)} %bitcast.11), calls=%async_computation | async-start | bytes 671744 | tf_op jit(solution)/shard_map/all_to_all | solution.py:178
  16.5 0.0 copy-done.1
  16.5 24.0 %all-gather = f32[256,128]{1,0:T(8,128)S(1)} all-gather(f32[16,128]{1,0:T(8,128)S(1)} %copy-done.1), channel_id=2, replica_groups=mesh['x'=4,'zl'=4,'c'=2,'y'=4,'zh'=4] {'x','y'}, dimensions={0}, use_global_device_ids=true | all-gather | bytes 139264 | tf_op jit(solution)/shard_map/all_gather | solution.py:180
  40.4 0.0 all-to-all-done
  40.4 1.9 %collective-permute-start = (f32[656,128]{1,0:T(8,128)S(1)}, f32[656,128]{1,0:T(8,128)S(1)}, u32[]{:S(2)}, u32[]{:S(2)}) collective-permute-start(f32[656,128]{1,0:T(8,128)S(1)} %bitcast.8), channel_id=1, source_target_pairs={{0,16},{16,0},{1,17},{17,1},{2,18},{18,2},{3,19},{19,3},{4,20},{20... | collective-permute-start | bytes 1007624 | tf_op jit(solution)/shard_map/ppermute | solution.py:179
  42.4 7.6 %block_first.1 = (f32[8,64,256]{2,1,0:T(8,128)S(1)}, bf16[8,128,256]{2,1,0:T(8,128)(2,1)S(1)}) custom-call(f32[16,16,128]{2,1,0:T(8,128)S(1)} %bitcast.10, f32[656,128]{1,0:T(8,128)S(1)} %bitcast.9), custom_call_target="tpu_custom_call" | custom-call | flops 8388608000 | bytes 335872 | tf_op jit(solution)/shard_map/block_first/pallas_call | solution.py:141
  50.0 0.0 collective-permute-done.refs_1_
  50.0 8.4 %block_last.1 = f32[16,32,128]{2,1,0:T(8,128)} custom-call(bf16[8,128,256]{2,1,0:T(8,128)(2,1)S(1)} %get-tuple-element.11.refs_0_, f32[656,128]{1,0:T(8,128)S(1)} %collective-permute-done.refs_1_, f32[8,64,256]{2,1,0:T(8,128)S(1)} %get-tuple-element.12.refs_2_), custom_call_target="tpu_custom_call" | custom-call | flops 8388608000 | bytes 335872 | tf_op jit(solution)/shard_map/block_last/pallas_call | solution.py:141
  58.4 6.2 %all-to-all-start.1 = ((f32[16,32,128]{2,1,0:T(8,128)}), f32[16,32,128]{2,1,0:T(8,128)S(1)}, u32[]{:S(2)}, u32[]{:S(2)}) async-start(f32[16,32,128]{2,1,0:T(8,128)} %block_last.1), calls=%async_computation.1 | async-start | bytes 524288 | tf_op jit(solution)/shard_map/all_to_all | solution.py:183
  65.2 0.0 copy-start
  65.3 8.5 %all-to-all-done.1 = f32[16,32,128]{2,1,0:T(8,128)S(1)} async-done(((f32[16,32,128]{2,1,0:T(8,128)}), f32[16,32,128]{2,1,0:T(8,128)S(1)}, u32[]{:S(2)}, u32[]{:S(2)}) %all-to-all-start.1) | async-done | bytes 262176 | tf_op jit(solution)/shard_map/all_to_all | solution.py:183
  73.8 0.0 copy-done
  73.8 0.6 multiply_add_fusion
  (1 shorter events, 0.0 us)
Async XLA Ops:
  1.6 14.9 %copy-start.1 = (f32[16,128]{1,0:T(8,128)S(1)}, f32[16,128]{1,0:T(8,128)}, u32[]{:S(2)}) copy-start(f32[16,128]{1,0:T(8,128)} %get-tuple-element.9) | copy-start | bytes 24580
  1.6 38.9 %all-to-all-start = ((f32[656,1,128]{2,1,0:T(1,128)}), f32[656,1,128]{2,1,0:T(1,128)S(1)}, u32[]{:S(2)}, u32[]{:S(2)}) async-start(f32[656,1,128]{2,1,0:T(1,128)} %bitcast.11), calls=%async_computation | async-start | bytes 671744 | tf_op jit(solution)/shard_map/all_to_all | solution.py:178
  40.4 9.5 %collective-permute-start = (f32[656,128]{1,0:T(8,128)S(1)}, f32[656,128]{1,0:T(8,128)S(1)}, u32[]{:S(2)}, u32[]{:S(2)}) collective-permute-start(f32[656,128]{1,0:T(8,128)S(1)} %bitcast.8), channel_id=1, source_target_pairs={{0,16},{16,0},{1,17},{17,1},{2,18},{18,2},{3,19},{19,3},{4,20},{20... | collective-permute-start | bytes 1007624 | tf_op jit(solution)/shard_map/ppermute | solution.py:179
  58.4 15.3 %all-to-all-start.1 = ((f32[16,32,128]{2,1,0:T(8,128)}), f32[16,32,128]{2,1,0:T(8,128)S(1)}, u32[]{:S(2)}, u32[]{:S(2)}) async-start(f32[16,32,128]{2,1,0:T(8,128)} %block_last.1), calls=%async_computation.1 | async-start | bytes 524288 | tf_op jit(solution)/shard_map/all_to_all | solution.py:183
  65.2 8.5 %copy-start = (f32[32,128]{1,0:T(8,128)S(1)}, f32[32,128]{1,0:T(8,128)}, u32[]{:S(2)}) copy-start(f32[32,128]{1,0:T(8,128)} %probes_ref.1) | copy-start | bytes 49156

commit v3 on v2

--- a/solution.py
+++ b/solution.py
@@ -72,6 +72,8 @@
     per = dims + n_probes
     n_rows, n_cols = a.shape[0] * TILE // LANES, cols_ref.shape[0] // per
     each = TILE // LANES
+    span = b.shape[1]
+    wide = span // LANES
     zero = jnp.zeros((UNIT, LANES), jnp.bfloat16)
 
     if not last:
@@ -84,15 +86,15 @@
         norm = jnp.sum(x * x, axis=0, keepdims=True)
         extended(-2.0 * x, jnp.ones_like(norm), norm, unit.at[s])
         v1, v2, v3 = split3(unit[s])
-        lanes = slice((s % each) * LANES, (s % each + 1) * LANES)
+        lanes = slice((s % wide) * LANES, (s % wide + 1) * LANES)
         stack = jnp.concatenate([v1, v2, v1, v2, v3, v1, zero, zero], axis=0)
-        b[s // each, lanes, :] = stack.T
+        b[s // wide, lanes, :] = stack.T
         p = cols_ref[s * per + dims : (s + 1) * per]
         p1 = p.astype(jnp.bfloat16)
         p2 = (p - p1.astype(jnp.float32)).astype(jnp.bfloat16)
         both = jnp.concatenate([p1, p2], axis=0)
-        q[s // each, :, lanes] = both
-        q[s // each, :, lanes.start + TILE : lanes.stop + TILE] = both
+        q[s // wide, :, lanes] = both
+        q[s // wide, :, lanes.start + span : lanes.stop + span] = both
     tiles, chunks = a.shape[0], b.shape[0]
     count = tiles * chunks
 
@@ -115,17 +117,22 @@
         for s in range(each):
             out_ref[tile * each + s] = value[:, s * LANES : (s + 1) * LANES]
 
+    def covariance(at, start, stop):
+        for r in range(start, stop, STEP):
+            high, low = halves(d[at % 2][r : r + STEP])
+            h[at % 2][r : r + STEP] = high
+            h[at % 2][span + r : span + r + STEP] = low
+
     d0[...] = distance(0)
     for at in range(count):
-        now, then = at % 2, 1 - at % 2
+        early = 0 if last or at == 0 else span // 2
         if at > 0:
-            add(at - 1, product(at - 1))
+            before = product(at - 1)
+            covariance(at, 0, early)
+            add(at - 1, before)
         if at + 1 < count:
-            d[then][...] = distance(at + 1)
-        for start in range(0, TILE, STEP):
-            high, low = halves(d[now][start : start + STEP])
-            h[now][start : start + STEP] = high
-            h[now][TILE + start : TILE + start + STEP] = low
+            d[1 - at % 2][...] = distance(at + 1)
+        covariance(at, early, span)
     add(count - 1, product(count - 1))
 
 
@@ -134,7 +141,8 @@
     last = total is not None
     n_rows = rows.shape[0] * TILE // LANES if last else rows.shape[0]
     n_cols = cols.shape[0] // (dims + n_probes)
-    row_tiles, col_tiles = n_rows * LANES // TILE, n_cols * LANES // TILE
+    span = 2 * TILE
+    row_tiles, col_tiles = n_rows * LANES // TILE, n_cols * LANES // span
     sums = jax.ShapeDtypeStruct((row_tiles, 2 * n_probes, TILE), f32)
     turned = jax.ShapeDtypeStruct((row_tiles, DEPTH, TILE), bf16)
     entries = n_rows * n_cols * LANES * LANES
@@ -144,13 +152,13 @@
         in_specs=[WHOLE] * (3 if last else 2),
         out_specs=WHOLE if last else (WHOLE, WHOLE),
         scratch_shapes=[
-            pltpu.VMEM((col_tiles, TILE, DEPTH), bf16),
-            pltpu.VMEM((col_tiles, 2 * n_probes, 2 * TILE), bf16),
+            pltpu.VMEM((col_tiles, span, DEPTH), bf16),
+            pltpu.VMEM((col_tiles, 2 * n_probes, 2 * span), bf16),
             pltpu.VMEM((n_cols, UNIT, LANES), f32),
-            pltpu.VMEM((TILE, TILE), f32),
-            pltpu.VMEM((TILE, TILE), f32),
-            pltpu.VMEM((2 * TILE, TILE), bf16),
-            pltpu.VMEM((2 * TILE, TILE), bf16),
+            pltpu.VMEM((span, TILE), f32),
+            pltpu.VMEM((span, TILE), f32),
+            pltpu.VMEM((2 * span, TILE), bf16),
+            pltpu.VMEM((2 * span, TILE), bf16),
         ]
         + [pltpu.VMEM(sums.shape, f32)] * last,
         compiler_params=pltpu.CompilerParams(vmem_limit_bytes=LIMIT),

time: 74.8 us -> 74.5 us (level)
  no operation moved by 1% of the time
where the time goes in v3:
time: 74.5 us; the launch traced here: 74 us
  blocking collectives  24 us (32%)
  starting transfers between devices  23 us (31%)
  Pallas kernels  17.3 us (23%)
  waiting for transfers between devices  8.51 us (11%)
    all_gather x1, blocking collectives, body(): rows = lax.all_gather(row, ROW_AXES, axis=0)  24 us
    pallas_call x2, Pallas kernels, block(): pl.pallas_call(functools.partial(block_kernel, last, dims), out_shape=jax...  15.7 us
    all_to_all x1, starting transfers between devices, body(): lax.all_to_all(cols.reshape(n_cols * per, 1, width), COL_AXES, 0, 0, tile...  14.9 us
    all_to_all x1, waiting for transfers between devices, body(): part = lax.all_to_all(part, ROW_AXES, 0, 0, tiled=True)  8.5 us
    all_to_all x1, starting transfers between devices, body(): part = lax.all_to_all(part, ROW_AXES, 0, 0, tiled=True)  6.17 us
    ppermute x1, starting transfers between devices, body(): other = lax.ppermute(cols, 'c', [(0, 1), (1, 0)])  1.92 us
    pallas_call x1, Pallas kernels, body(): pl.pallas_call(prepare_kernel, out_shape=(jax.ShapeDtypeStruct((UNIT, wid...  1.58 us
  transfers between devices with their start and end apart: 3, of which 1 were waited for; matrix products, arithmetic and copies ran while one was open for 0% of the time, Pallas kernels for 10%

profile of v3, /device:TPU:64, one launch (start us, length us, event | category | flops | bytes accessed | tf_op | source)
XLA Modules:
  0.0 74.0 jit_solution(15295014004188611794)
XLA Ops:
  0.0 1.6 %prepare.1 = (f32[16,128]{1,0:T(8,128)}, f32[656,128]{1,0:T(8,128)}) custom-call(f32[9,128]{1,0:T(8,128)} %points_ref.1, f32[1,9]{1,0:T(1,128)} %bitcast.12, f32[32,128]{1,0:T(8,128)} %probes_ref.1), custom_call_target="tpu_custom_call" | custom-call | tf_op jit(solution)/shard_map/prepare/pallas_call | solution.py:175
  1.6 0.0 copy-start.1
  1.6 14.9 %all-to-all-start = ((f32[656,1,128]{2,1,0:T(1,128)}), f32[656,1,128]{2,1,0:T(1,128)S(1)}, u32[]{:S(2)}, u32[]{:S(2)}) async-start(f32[656,1,128]{2,1,0:T(1,128)} %bitcast.11), calls=%async_computation | async-start | bytes 671744 | tf_op jit(solution)/shard_map/all_to_all | solution.py:186
  16.5 0.0 copy-done.1
  16.5 24.0 %all-gather = f32[256,128]{1,0:T(8,128)S(1)} all-gather(f32[16,128]{1,0:T(8,128)S(1)} %copy-done.1), channel_id=2, replica_groups=mesh['x'=4,'zl'=4,'c'=2,'y'=4,'zh'=4] {'x','y'}, dimensions={0}, use_global_device_ids=true | all-gather | bytes 139264 | tf_op jit(solution)/shard_map/all_gather | solution.py:188
  40.4 0.0 all-to-all-done
  40.4 1.9 %collective-permute-start = (f32[656,128]{1,0:T(8,128)S(1)}, f32[656,128]{1,0:T(8,128)S(1)}, u32[]{:S(2)}, u32[]{:S(2)}) collective-permute-start(f32[656,128]{1,0:T(8,128)S(1)} %bitcast.8), channel_id=1, source_target_pairs={{0,16},{16,0},{1,17},{17,1},{2,18},{18,2},{3,19},{19,3},{4,20},{20... | collective-permute-start | bytes 1007624 | tf_op jit(solution)/shard_map/ppermute | solution.py:187
  42.4 7.4 %block_first.1 = (f32[8,64,256]{2,1,0:T(8,128)S(1)}, bf16[8,128,256]{2,1,0:T(8,128)(2,1)S(1)}) custom-call(f32[16,16,128]{2,1,0:T(8,128)S(1)} %bitcast.10, f32[656,128]{1,0:T(8,128)S(1)} %bitcast.9), custom_call_target="tpu_custom_call" | custom-call | flops 8388608000 | bytes 335872 | tf_op jit(solution)/shard_map/block_first/pallas_call | solution.py:149
  49.8 0.0 collective-permute-done.refs_1_
  49.8 8.3 %block_last.1 = f32[16,32,128]{2,1,0:T(8,128)} custom-call(bf16[8,128,256]{2,1,0:T(8,128)(2,1)S(1)} %get-tuple-element.11.refs_0_, f32[656,128]{1,0:T(8,128)S(1)} %collective-permute-done.refs_1_, f32[8,64,256]{2,1,0:T(8,128)S(1)} %get-tuple-element.12.refs_2_), custom_call_target="tpu_custom_call" | custom-call | flops 8388608000 | bytes 335872 | tf_op jit(solution)/shard_map/block_last/pallas_call | solution.py:149
  58.1 6.2 %all-to-all-start.1 = ((f32[16,32,128]{2,1,0:T(8,128)}), f32[16,32,128]{2,1,0:T(8,128)S(1)}, u32[]{:S(2)}, u32[]{:S(2)}) async-start(f32[16,32,128]{2,1,0:T(8,128)} %block_last.1), calls=%async_computation.1 | async-start | bytes 524288 | tf_op jit(solution)/shard_map/all_to_all | solution.py:191
  64.9 0.0 copy-start
  64.9 8.5 %all-to-all-done.1 = f32[16,32,128]{2,1,0:T(8,128)S(1)} async-done(((f32[16,32,128]{2,1,0:T(8,128)}), f32[16,32,128]{2,1,0:T(8,128)S(1)}, u32[]{:S(2)}, u32[]{:S(2)}) %all-to-all-start.1) | async-done | bytes 262176 | tf_op jit(solution)/shard_map/all_to_all | solution.py:191
  73.4 0.0 copy-done
  73.4 0.6 multiply_add_fusion
  (1 shorter events, 0.0 us)
Async XLA Ops:
  1.6 14.9 %copy-start.1 = (f32[16,128]{1,0:T(8,128)S(1)}, f32[16,128]{1,0:T(8,128)}, u32[]{:S(2)}) copy-start(f32[16,128]{1,0:T(8,128)} %get-tuple-element.9) | copy-start | bytes 24580
  1.6 38.9 %all-to-all-start = ((f32[656,1,128]{2,1,0:T(1,128)}), f32[656,1,128]{2,1,0:T(1,128)S(1)}, u32[]{:S(2)}, u32[]{:S(2)}) async-start(f32[656,1,128]{2,1,0:T(1,128)} %bitcast.11), calls=%async_computation | async-start | bytes 671744 | tf_op jit(solution)/shard_map/all_to_all | solution.py:186
  40.4 9.3 %collective-permute-start = (f32[656,128]{1,0:T(8,128)S(1)}, f32[656,128]{1,0:T(8,128)S(1)}, u32[]{:S(2)}, u32[]{:S(2)}) collective-permute-start(f32[656,128]{1,0:T(8,128)S(1)} %bitcast.8), channel_id=1, source_target_pairs={{0,16},{16,0},{1,17},{17,1},{2,18},{18,2},{3,19},{19,3},{4,20},{20... | collective-permute-start | bytes 1007624 | tf_op jit(solution)/shard_map/ppermute | solution.py:187
  58.1 15.3 %all-to-all-start.1 = ((f32[16,32,128]{2,1,0:T(8,128)}), f32[16,32,128]{2,1,0:T(8,128)S(1)}, u32[]{:S(2)}, u32[]{:S(2)}) async-start(f32[16,32,128]{2,1,0:T(8,128)} %block_last.1), calls=%async_computation.1 | async-start | bytes 524288 | tf_op jit(solution)/shard_map/all_to_all | solution.py:191
  64.9 8.5 %copy-start = (f32[32,128]{1,0:T(8,128)S(1)}, f32[32,128]{1,0:T(8,128)}, u32[]{:S(2)}) copy-start(f32[32,128]{1,0:T(8,128)} %probes_ref.1) | copy-start | bytes 49156

commit v4 on v3

--- a/solution.py
+++ b/solution.py
@@ -141,7 +141,7 @@
     last = total is not None
     n_rows = rows.shape[0] * TILE // LANES if last else rows.shape[0]
     n_cols = cols.shape[0] // (dims + n_probes)
-    span = 2 * TILE
+    span = 4 * TILE
     row_tiles, col_tiles = n_rows * LANES // TILE, n_cols * LANES // span
     sums = jax.ShapeDtypeStruct((row_tiles, 2 * n_probes, TILE), f32)
     turned = jax.ShapeDtypeStruct((row_tiles, DEPTH, TILE), bf16)

time: 74.5 us -> 74.4 us (level)
  no operation moved by 1% of the time
where the time goes in v4:
time: 74.4 us; the launch traced here: 74 us
  blocking collectives  24 us (32%)
  starting transfers between devices  23 us (31%)
  Pallas kernels  17.2 us (23%)
  waiting for transfers between devices  8.51 us (11%)
    all_gather x1, blocking collectives, body(): rows = lax.all_gather(row, ROW_AXES, axis=0)  24 us
    pallas_call x2, Pallas kernels, block(): pl.pallas_call(functools.partial(block_kernel, last, dims), out_shape=jax...  15.7 us
    all_to_all x1, starting transfers between devices, body(): lax.all_to_all(cols.reshape(n_cols * per, 1, width), COL_AXES, 0, 0, tile...  14.9 us
    all_to_all x1, waiting for transfers between devices, body(): part = lax.all_to_all(part, ROW_AXES, 0, 0, tiled=True)  8.51 us
    all_to_all x1, starting transfers between devices, body(): part = lax.all_to_all(part, ROW_AXES, 0, 0, tiled=True)  6.16 us
    ppermute x1, starting transfers between devices, body(): other = lax.ppermute(cols, 'c', [(0, 1), (1, 0)])  1.92 us
    pallas_call x1, Pallas kernels, body(): pl.pallas_call(prepare_kernel, out_shape=(jax.ShapeDtypeStruct((UNIT, wid...  1.58 us
  transfers between devices with their start and end apart: 3, of which 1 were waited for; matrix products, arithmetic and copies ran while one was open for 0% of the time, Pallas kernels for 10%

profile of v4, /device:TPU:64, one launch (start us, length us, event | category | flops | bytes accessed | tf_op | source)
XLA Modules:
  0.0 74.0 jit_solution(10041858667853671643)
XLA Ops:
  0.0 1.6 %prepare.1 = (f32[16,128]{1,0:T(8,128)}, f32[656,128]{1,0:T(8,128)}) custom-call(f32[9,128]{1,0:T(8,128)} %points_ref.1, f32[1,9]{1,0:T(1,128)} %bitcast.12, f32[32,128]{1,0:T(8,128)} %probes_ref.1), custom_call_target="tpu_custom_call" | custom-call | tf_op jit(solution)/shard_map/prepare/pallas_call | solution.py:175
  1.6 0.0 copy-start.1
  1.6 14.9 %all-to-all-start = ((f32[656,1,128]{2,1,0:T(1,128)}), f32[656,1,128]{2,1,0:T(1,128)S(1)}, u32[]{:S(2)}, u32[]{:S(2)}) async-start(f32[656,1,128]{2,1,0:T(1,128)} %bitcast.11), calls=%async_computation | async-start | bytes 671744 | tf_op jit(solution)/shard_map/all_to_all | solution.py:186
  16.5 0.0 copy-done.1
  16.5 24.0 %all-gather = f32[256,128]{1,0:T(8,128)S(1)} all-gather(f32[16,128]{1,0:T(8,128)S(1)} %copy-done.1), channel_id=2, replica_groups=mesh['x'=4,'zl'=4,'c'=2,'y'=4,'zh'=4] {'x','y'}, dimensions={0}, use_global_device_ids=true | all-gather | bytes 139264 | tf_op jit(solution)/shard_map/all_gather | solution.py:188
  40.4 0.0 all-to-all-done
  40.4 1.9 %collective-permute-start = (f32[656,128]{1,0:T(8,128)S(1)}, f32[656,128]{1,0:T(8,128)S(1)}, u32[]{:S(2)}, u32[]{:S(2)}) collective-permute-start(f32[656,128]{1,0:T(8,128)S(1)} %bitcast.8), channel_id=1, source_target_pairs={{0,16},{16,0},{1,17},{17,1},{2,18},{18,2},{3,19},{19,3},{4,20},{20... | collective-permute-start | bytes 1007624 | tf_op jit(solution)/shard_map/ppermute | solution.py:187
  42.4 7.4 %block_first.1 = (f32[8,64,256]{2,1,0:T(8,128)S(1)}, bf16[8,128,256]{2,1,0:T(8,128)(2,1)S(1)}) custom-call(f32[16,16,128]{2,1,0:T(8,128)S(1)} %bitcast.10, f32[656,128]{1,0:T(8,128)S(1)} %bitcast.9), custom_call_target="tpu_custom_call" | custom-call | flops 8388608000 | bytes 335872 | tf_op jit(solution)/shard_map/block_first/pallas_call | solution.py:149
  49.8 0.0 collective-permute-done.refs_1_
  49.8 8.2 %block_last.1 = f32[16,32,128]{2,1,0:T(8,128)} custom-call(bf16[8,128,256]{2,1,0:T(8,128)(2,1)S(1)} %get-tuple-element.11.refs_0_, f32[656,128]{1,0:T(8,128)S(1)} %collective-permute-done.refs_1_, f32[8,64,256]{2,1,0:T(8,128)S(1)} %get-tuple-element.12.refs_2_), custom_call_target="tpu_custom_call" | custom-call | flops 8388608000 | bytes 335872 | tf_op jit(solution)/shard_map/block_last/pallas_call | solution.py:149
  58.0 6.2 %all-to-all-start.1 = ((f32[16,32,128]{2,1,0:T(8,128)}), f32[16,32,128]{2,1,0:T(8,128)S(1)}, u32[]{:S(2)}, u32[]{:S(2)}) async-start(f32[16,32,128]{2,1,0:T(8,128)} %block_last.1), calls=%async_computation.1 | async-start | bytes 524288 | tf_op jit(solution)/shard_map/all_to_all | solution.py:191
  64.8 0.0 copy-start
  64.9 8.5 %all-to-all-done.1 = f32[16,32,128]{2,1,0:T(8,128)S(1)} async-done(((f32[16,32,128]{2,1,0:T(8,128)}), f32[16,32,128]{2,1,0:T(8,128)S(1)}, u32[]{:S(2)}, u32[]{:S(2)}) %all-to-all-start.1) | async-done | bytes 262176 | tf_op jit(solution)/shard_map/all_to_all | solution.py:191
  73.4 0.0 copy-done
  73.4 0.6 multiply_add_fusion
  (1 shorter events, 0.0 us)
Async XLA Ops:
  1.6 14.9 %copy-start.1 = (f32[16,128]{1,0:T(8,128)S(1)}, f32[16,128]{1,0:T(8,128)}, u32[]{:S(2)}) copy-start(f32[16,128]{1,0:T(8,128)} %get-tuple-element.9) | copy-start | bytes 24580
  1.6 38.9 %all-to-all-start = ((f32[656,1,128]{2,1,0:T(1,128)}), f32[656,1,128]{2,1,0:T(1,128)S(1)}, u32[]{:S(2)}, u32[]{:S(2)}) async-start(f32[656,1,128]{2,1,0:T(1,128)} %bitcast.11), calls=%async_computation | async-start | bytes 671744 | tf_op jit(solution)/shard_map/all_to_all | solution.py:186
  40.4 9.4 %collective-permute-start = (f32[656,128]{1,0:T(8,128)S(1)}, f32[656,128]{1,0:T(8,128)S(1)}, u32[]{:S(2)}, u32[]{:S(2)}) collective-permute-start(f32[656,128]{1,0:T(8,128)S(1)} %bitcast.8), channel_id=1, source_target_pairs={{0,16},{16,0},{1,17},{17,1},{2,18},{18,2},{3,19},{19,3},{4,20},{20... | collective-permute-start | bytes 1007624 | tf_op jit(solution)/shard_map/ppermute | solution.py:187
  58.0 15.3 %all-to-all-start.1 = ((f32[16,32,128]{2,1,0:T(8,128)}), f32[16,32,128]{2,1,0:T(8,128)S(1)}, u32[]{:S(2)}, u32[]{:S(2)}) async-start(f32[16,32,128]{2,1,0:T(8,128)} %block_last.1), calls=%async_computation.1 | async-start | bytes 524288 | tf_op jit(solution)/shard_map/all_to_all | solution.py:191
  64.8 8.5 %copy-start = (f32[32,128]{1,0:T(8,128)S(1)}, f32[32,128]{1,0:T(8,128)}, u32[]{:S(2)}) copy-start(f32[32,128]{1,0:T(8,128)} %probes_ref.1) | copy-start | bytes 49156

commit v5 on v4

--- a/solution.py
+++ b/solution.py
@@ -141,7 +141,7 @@
     last = total is not None
     n_rows = rows.shape[0] * TILE // LANES if last else rows.shape[0]
     n_cols = cols.shape[0] // (dims + n_probes)
-    span = 4 * TILE
+    span = 4 * TILE if last else 2 * TILE
     row_tiles, col_tiles = n_rows * LANES // TILE, n_cols * LANES // span
     sums = jax.ShapeDtypeStruct((row_tiles, 2 * n_probes, TILE), f32)
     turned = jax.ShapeDtypeStruct((row_tiles, DEPTH, TILE), bf16)

time: 74.4 us -> 74.4 us (level)
  no operation moved by 1% of the time
where the time goes in v5:
time: 74.4 us; the launch traced here: 74 us
  blocking collectives  24 us (32%)
  starting transfers between devices  23 us (31%)
  Pallas kernels  17.2 us (23%)
  waiting for transfers between devices  8.51 us (11%)
    all_gather x1, blocking collectives, body(): rows = lax.all_gather(row, ROW_AXES, axis=0)  24 us
    pallas_call x2, Pallas kernels, block(): pl.pallas_call(functools.partial(block_kernel, last, dims), out_shape=jax...  15.6 us
    all_to_all x1, starting transfers between devices, body(): lax.all_to_all(cols.reshape(n_cols * per, 1, width), COL_AXES, 0, 0, tile...  14.9 us
    all_to_all x1, waiting for transfers between devices, body(): part = lax.all_to_all(part, ROW_AXES, 0, 0, tiled=True)  8.5 us
    all_to_all x1, starting transfers between devices, body(): part = lax.all_to_all(part, ROW_AXES, 0, 0, tiled=True)  6.17 us
    ppermute x1, starting transfers between devices, body(): other = lax.ppermute(cols, 'c', [(0, 1), (1, 0)])  1.92 us
    pallas_call x1, Pallas kernels, body(): pl.pallas_call(prepare_kernel, out_shape=(jax.ShapeDtypeStruct((UNIT, wid...  1.58 us
  transfers between devices with their start and end apart: 3, of which 1 were waited for; matrix products, arithmetic and copies ran while one was open for 0% of the time, Pallas kernels for 10%

profile of v5, /device:TPU:64, one launch (start us, length us, event | category | flops | bytes accessed | tf_op | source)
XLA Modules:
  0.0 74.0 jit_solution(16797957373662752599)
XLA Ops:
  0.0 1.6 %prepare.1 = (f32[16,128]{1,0:T(8,128)}, f32[656,128]{1,0:T(8,128)}) custom-call(f32[9,128]{1,0:T(8,128)} %points_ref.1, f32[1,9]{1,0:T(1,128)} %bitcast.12, f32[32,128]{1,0:T(8,128)} %probes_ref.1), custom_call_target="tpu_custom_call" | custom-call | tf_op jit(solution)/shard_map/prepare/pallas_call | solution.py:175
  1.6 0.0 copy-start.1
  1.6 14.9 %all-to-all-start = ((f32[656,1,128]{2,1,0:T(1,128)}), f32[656,1,128]{2,1,0:T(1,128)S(1)}, u32[]{:S(2)}, u32[]{:S(2)}) async-start(f32[656,1,128]{2,1,0:T(1,128)} %bitcast.11), calls=%async_computation | async-start | bytes 671744 | tf_op jit(solution)/shard_map/all_to_all | solution.py:186
  16.5 0.0 copy-done.1
  16.5 24.0 %all-gather = f32[256,128]{1,0:T(8,128)S(1)} all-gather(f32[16,128]{1,0:T(8,128)S(1)} %copy-done.1), channel_id=2, replica_groups=mesh['x'=4,'zl'=4,'c'=2,'y'=4,'zh'=4] {'x','y'}, dimensions={0}, use_global_device_ids=true | all-gather | bytes 139264 | tf_op jit(solution)/shard_map/all_gather | solution.py:188
  40.4 0.0 all-to-all-done
  40.4 1.9 %collective-permute-start = (f32[656,128]{1,0:T(8,128)S(1)}, f32[656,128]{1,0:T(8,128)S(1)}, u32[]{:S(2)}, u32[]{:S(2)}) collective-permute-start(f32[656,128]{1,0:T(8,128)S(1)} %bitcast.8), channel_id=1, source_target_pairs={{0,16},{16,0},{1,17},{17,1},{2,18},{18,2},{3,19},{19,3},{4,20},{20... | collective-permute-start | bytes 1007624 | tf_op jit(solution)/shard_map/ppermute | solution.py:187
  42.4 7.4 %block_first.1 = (f32[8,64,256]{2,1,0:T(8,128)S(1)}, bf16[8,128,256]{2,1,0:T(8,128)(2,1)S(1)}) custom-call(f32[16,16,128]{2,1,0:T(8,128)S(1)} %bitcast.10, f32[656,128]{1,0:T(8,128)S(1)} %bitcast.9), custom_call_target="tpu_custom_call" | custom-call | flops 8388608000 | bytes 335872 | tf_op jit(solution)/shard_map/block_first/pallas_call | solution.py:149
  49.8 0.0 collective-permute-done.refs_1_
  49.8 8.2 %block_last.1 = f32[16,32,128]{2,1,0:T(8,128)} custom-call(bf16[8,128,256]{2,1,0:T(8,128)(2,1)S(1)} %get-tuple-element.11.refs_0_, f32[656,128]{1,0:T(8,128)S(1)} %collective-permute-done.refs_1_, f32[8,64,256]{2,1,0:T(8,128)S(1)} %get-tuple-element.12.refs_2_), custom_call_target="tpu_custom_call" | custom-call | flops 8388608000 | bytes 335872 | tf_op jit(solution)/shard_map/block_last/pallas_call | solution.py:149
  58.0 6.2 %all-to-all-start.1 = ((f32[16,32,128]{2,1,0:T(8,128)}), f32[16,32,128]{2,1,0:T(8,128)S(1)}, u32[]{:S(2)}, u32[]{:S(2)}) async-start(f32[16,32,128]{2,1,0:T(8,128)} %block_last.1), calls=%async_computation.1 | async-start | bytes 524288 | tf_op jit(solution)/shard_map/all_to_all | solution.py:191
  64.8 0.0 copy-start
  64.8 8.5 %all-to-all-done.1 = f32[16,32,128]{2,1,0:T(8,128)S(1)} async-done(((f32[16,32,128]{2,1,0:T(8,128)}), f32[16,32,128]{2,1,0:T(8,128)S(1)}, u32[]{:S(2)}, u32[]{:S(2)}) %all-to-all-start.1) | async-done | bytes 262176 | tf_op jit(solution)/shard_map/all_to_all | solution.py:191
  73.4 0.0 copy-done
  73.4 0.6 multiply_add_fusion
  (1 shorter events, 0.0 us)
Async XLA Ops:
  1.6 14.9 %copy-start.1 = (f32[16,128]{1,0:T(8,128)S(1)}, f32[16,128]{1,0:T(8,128)}, u32[]{:S(2)}) copy-start(f32[16,128]{1,0:T(8,128)} %get-tuple-element.9) | copy-start | bytes 24580
  1.6 38.9 %all-to-all-start = ((f32[656,1,128]{2,1,0:T(1,128)}), f32[656,1,128]{2,1,0:T(1,128)S(1)}, u32[]{:S(2)}, u32[]{:S(2)}) async-start(f32[656,1,128]{2,1,0:T(1,128)} %bitcast.11), calls=%async_computation | async-start | bytes 671744 | tf_op jit(solution)/shard_map/all_to_all | solution.py:186
  40.4 9.3 %collective-permute-start = (f32[656,128]{1,0:T(8,128)S(1)}, f32[656,128]{1,0:T(8,128)S(1)}, u32[]{:S(2)}, u32[]{:S(2)}) collective-permute-start(f32[656,128]{1,0:T(8,128)S(1)} %bitcast.8), channel_id=1, source_target_pairs={{0,16},{16,0},{1,17},{17,1},{2,18},{18,2},{3,19},{19,3},{4,20},{20... | collective-permute-start | bytes 1007624 | tf_op jit(solution)/shard_map/ppermute | solution.py:187
  58.0 15.3 %all-to-all-start.1 = ((f32[16,32,128]{2,1,0:T(8,128)}), f32[16,32,128]{2,1,0:T(8,128)S(1)}, u32[]{:S(2)}, u32[]{:S(2)}) async-start(f32[16,32,128]{2,1,0:T(8,128)} %block_last.1), calls=%async_computation.1 | async-start | bytes 524288 | tf_op jit(solution)/shard_map/all_to_all | solution.py:191
  64.8 8.5 %copy-start = (f32[32,128]{1,0:T(8,128)S(1)}, f32[32,128]{1,0:T(8,128)}, u32[]{:S(2)}) copy-start(f32[32,128]{1,0:T(8,128)} %probes_ref.1) | copy-start | bytes 49156
